TPU v7x, 512 devices: a whole 4x8x8 slice. The times are simulated.
512 devices in a mesh: space: 64 (over x, z, y_lo), ens: 8 (over y_hi, core).
Axes of the slice: x: 4, y: 8 (y_hi: 4, y_lo: 2; y = y_hi * 2 + y_lo), z: 8, core: 2. Of those that a mesh axis runs over, the one named last changes fastest.
Arguments:
- state: bfloat16 [8, 16, 1024, 384], P('ens', None, 'space'), may hold values from -6 to 6
- cotangent: bfloat16 [8, 16, 1024, 384], P('ens', None, 'space'), may hold values from -6 to 6
- halo_cols: int32 [16], replicated, may hold values from 1 to 16, as said below
- row_offset: int32 [16, 4], replicated, may hold values from -2 to 2
- conv_weight: float32 [4, 384], replicated, may hold values from -4 to 4
- norm_gain: float32 [384], replicated, may hold values from 0.5 to 1.5
- weight_in: bfloat16 [384, 768], replicated, may hold values from -0.3125 to 0.3125
- weight_out: bfloat16 [768, 384], replicated, may hold values from -0.21875 to 0.21875
Outputs:
- grad_state: bfloat16 [8, 16, 1024, 384], P('ens', None, 'space')
- grad_conv: float32 [4, 384], replicated
- grad_gain: float32 [384], replicated
- grad_in: bfloat16 [384, 768], replicated
- grad_out: bfloat16 [768, 384], replicated
Inputs may be any that keep to these rules, and one draw needn't show every extreme that they name: halo_cols rises with the row index, within one of a straight rise from 1 at row 0 to 16 at the last row, which is the polar one.
All inputs are finite; a program needn't handle non-finite values.
Results may differ from a plain program's by a relative error of at most 0.0078.
Values may be sent and summed in bfloat16 or wider, within the bound.
No kernel may reach another device: no remote copies, remote signals or barrier semaphores. Data moves between devices by JAX's collectives and lax.ppermute only.
A program may use at most 64 MiB of HBM per device.

v0:
```python
import math

import jax
import jax.numpy as jnp
from jax import lax
from jax.sharding import PartitionSpec as P

K = 4
HMAX = 16


norm_eps = 1e-05


def padded(cells, sides, width):
    for axis, dim in sides:
        count = lax.axis_size(axis)
        head = lax.slice_in_dim(cells, 0, width, axis=dim)
        tail = lax.slice_in_dim(cells, cells.shape[dim] - width, cells.shape[dim], axis=dim)
        cells = jnp.concatenate(
            [
                lax.ppermute(tail, axis, [(i, (i + 1) % count) for i in range(count)]),
                cells,
                lax.ppermute(head, axis, [((i + 1) % count, i) for i in range(count)]),
            ],
            axis=dim,
        )
    return cells


def from_behind(value, axis, by):
    peers = lax.axis_size(axis)
    return lax.ppermute(value, axis, [(i, (i + by) % peers) for i in range(peers)])


def basis_profiles(halo_cols):
    steps_off = jnp.arange(2 * HMAX + 1, dtype=jnp.int32) - HMAX
    reach = halo_cols.astype(jnp.float32)[:, None]
    ratio = steps_off.astype(jnp.float32)[None, :] / (reach + 1.0)
    inside = jnp.abs(steps_off)[None, :] <= halo_cols[:, None]
    base = jnp.where(inside, (1.0 - ratio * ratio) / jnp.sqrt(reach + 1.0), jnp.zeros_like(ratio))
    return jnp.stack([base * ratio**power for power in range(K)], axis=1).astype(jnp.bfloat16)


def band_matrix(profile, spread):
    valid = (spread >= 0) & (spread <= 2 * HMAX)
    picked = profile[:, :, jnp.clip(spread, 0, 2 * HMAX)]
    return jnp.where(valid[None, None], picked, jnp.zeros_like(picked))


def pick_rows(values, offsets):
    row_count = values.shape[0]
    source = jnp.arange(row_count, dtype=jnp.int32) + offsets
    valid = (source >= 0) & (source < row_count)
    picked = values[jnp.clip(source, 0, row_count - 1)]
    return jnp.where(valid[:, None, None], picked, jnp.zeros_like(picked))


def sum_rows(values, offsets):
    row_count = values.shape[0]
    source = jnp.arange(row_count, dtype=jnp.int32) + offsets
    valid = (source >= 0) & (source < row_count)
    targets = jnp.where(valid, source, row_count)
    return jax.ops.segment_sum(values, targets, num_segments=row_count + 1)[:row_count]


def contract_cells(left, right):
    return lax.dot_general(
        left, right, (((0,), (0,)), ((), ())), preferred_element_type=jnp.float32
    )


def contract_features(left, right):
    return lax.dot_general(
        left, right, (((1,), (1,)), ((), ())), preferred_element_type=jnp.float32
    )


def on_device(
    state, cotangent, halo_cols, row_offset, conv_weight, norm_gain, weight_in, weight_out
):
    local_state = state[0]
    local_grad = cotangent[0]
    row_count, col_count, channels = local_state.shape
    padded_cols = col_count + 2 * HMAX
    profile = basis_profiles(halo_cols)
    spread = (
        jnp.arange(padded_cols, dtype=jnp.int32)[None, :]
        - jnp.arange(col_count, dtype=jnp.int32)[:, None]
    )
    forward_band = band_matrix(profile, spread)
    extended = padded(local_state, (("space", 1),), HMAX)
    layers = []
    for basis_id in range(K):
        picked = pick_rows(extended, row_offset[:, basis_id])
        layers.append(
            jnp.einsum(
                "rjl,rlc->rjc",
                forward_band[:, basis_id],
                picked,
                preferred_element_type=jnp.float32,
            )
        )
    responses = jnp.stack(layers)
    filtered = jnp.sum(conv_weight[:, None, None, :] * responses, axis=0)
    cell_count = row_count * col_count
    flat_mixed = filtered.reshape(cell_count, channels)
    center = jnp.mean(flat_mixed, axis=-1, keepdims=True)
    offset_vals = flat_mixed - center
    variance = jnp.mean(offset_vals * offset_vals, axis=-1, keepdims=True)
    inverse = 1.0 / jnp.sqrt(variance + norm_eps)
    normed = offset_vals * inverse
    scaled = (normed * norm_gain).astype(jnp.bfloat16)
    preact = jnp.dot(scaled, weight_in, preferred_element_type=jnp.float32)
    hidden_vals, gelu_back = jax.vjp(jax.nn.gelu, preact)
    hidden = hidden_vals.astype(jnp.bfloat16)
    flat_grad = local_grad.reshape(cell_count, channels)
    factor = 1.0 / math.sqrt(lax.axis_size("ens") * cell_count * lax.axis_size("space"))
    out_term = contract_cells(hidden, flat_grad)
    grad_hidden = contract_features(flat_grad, weight_out)
    grad_preact = gelu_back(grad_hidden)[0].astype(jnp.bfloat16)
    in_term = contract_cells(scaled, grad_preact)
    grad_scaled = contract_features(grad_preact, weight_in)
    gain_term = jnp.sum(grad_scaled * normed, axis=0)
    grad_normed = grad_scaled * norm_gain
    grad_filtered = (
        grad_normed
        - jnp.mean(grad_normed, axis=-1, keepdims=True)
        - normed * jnp.mean(grad_normed * normed, axis=-1, keepdims=True)
    ) * inverse
    grad_field = grad_filtered.reshape(row_count, col_count, channels)
    conv_term = jnp.sum(grad_field[None] * responses, axis=(1, 2))
    grad_rounded = grad_field.astype(jnp.bfloat16)
    spread_out = jnp.zeros((row_count, padded_cols, channels), jnp.float32)
    for basis_id in range(K):
        part_sum = (
            jnp.einsum(
                "rjl,rjc->rlc",
                forward_band[:, basis_id],
                grad_rounded,
                preferred_element_type=jnp.float32,
            )
            * conv_weight[basis_id]
        )
        spread_out = spread_out + sum_rows(part_sum, row_offset[:, basis_id])
    from_east = from_behind(spread_out[:, :HMAX].astype(jnp.bfloat16), "space", -1).astype(
        jnp.float32
    )
    from_west = from_behind(
        spread_out[:, col_count + HMAX :].astype(jnp.bfloat16), "space", 1
    ).astype(jnp.float32)
    interior = spread_out[:, HMAX : HMAX + col_count]
    interior = interior.at[:, :HMAX].add(from_west)
    interior = interior.at[:, col_count - HMAX :].add(from_east)
    grad_state = (local_grad.astype(jnp.float32) + interior).astype(jnp.bfloat16)[None]
    conv_total, gain_total, in_total, out_total = lax.psum(
        (conv_term, gain_term, in_term, out_term), ("space", "ens")
    )
    grad_conv = conv_total * factor
    grad_gain = gain_total * factor
    grad_in = (in_total * factor).astype(jnp.bfloat16)
    grad_out = (out_total * factor).astype(jnp.bfloat16)
    return (grad_state, grad_conv, grad_gain, grad_in, grad_out)


def solution(mesh):
    return jax.shard_map(
        on_device,
        mesh=mesh,
        in_specs=(
            P("ens", None, "space", None),
            P("ens", None, "space", None),
            P(),
            P(),
            P(),
            P(),
            P(),
            P(),
        ),
        out_specs=(P("ens", None, "space", None), P(), P(), P(), P()),
        check_vma=False,
    )
```

profile of v0, /device:TPU:1, one launch (start us, length us, event | category | flops | bytes accessed | tf_op | source)
XLA Modules:
  0.0 341.8 jit_solution(12435922543105120971)
XLA Ops:
  7.2 14.8 %collective-permute-start.1 = (bf16[16,16,384]{2,1,0:T(8,128)(2,1)}, bf16[16,16,384]{2,1,0:T(8,128)(2,1)S(1)}, u32[]{:S(2)}, u32[]{:S(2)}) collective-permute-start(bf16[16,16,384]{2,1,0:T(8,128)(2,1)} %bitcast.100), channel_id=1, source_target_pairs={{8,0},{16,8},{24,16},{32,24},{40,32},{48,40},{56,48},{64,56},{72,6... | collective-permute-start | bytes 589832 | tf_op jit(solution)/shard_map/ppermute | solution.py:24
  22.1 1.9 collective-permute-start
  27.4 2.8 gather_fusion
  32.3 1.6 collective-permute-done
  34.6 1.4 gather_fusion.3
  36.1 1.4 gather_fusion.2
  38.5 1.4 convolution_bitcast_fusion.1
  41.6 1.8 fusion.6
  44.0 1.4 fusion.59
  45.3 1.5 fusion.15
  47.8 1.4 convolution_multiply_fusion
  49.2 1.5 convolution_multiply_fusion.1
  51.9 2.2 convolution_multiply_fusion.3
  54.3 1.7 scatter_fusion.1
  56.1 2.7 scatter_fusion.2
  60.1 3.9 %scatter_fusion.3 = f32[17,48,384]{2,1,0:T(8,128)} fusion(f32[17,48,384]{2,1,0:T(8,128)} %broadcast.571.clone, s32[16]{0:T(128)S(1)} %get-tuple-element.75, f32[16,48,384]{2,1,0:T(8,128)} %convolution_multiply_fusion), kind=kCustom, calls=%fused_computation.8 | custom fusion | flops 294912 | bytes 3539008 | tf_op jit(solution)/shard_map/scatter-add | solution.py:64
  64.2 2.7 scatter_fusion
  67.0 3.2 fusion.56
  70.2 2.1 collective-permute-start.2
  72.3 7.6 %collective-permute-start.3 = (bf16[16,16,384]{2,1,0:T(8,128)(2,1)S(1)}, bf16[16,16,384]{2,1,0:T(8,128)(2,1)S(1)}, u32[]{:S(2)}, u32[]{:S(2)}) collective-permute-start(bf16[16,16,384]{2,1,0:T(8,128)(2,1)S(1)} %get-tuple-element.63), channel_id=1, source_target_pairs={{0,504},{8,0},{16,8},{24,16},{32,24},{40,32},{48,40},{56,48},{64,5... | collective-permute-start | bytes 589832 | tf_op jit(solution)/shard_map/ppermute | solution.py:33
  80.0 96.4 %all-reduce = (f32[4,384]{1,0:T(4,128)S(1)}, f32[384]{0:T(512)S(1)}) all-reduce(f32[4,384]{1,0:T(4,128)S(1)} %multiply_reduce_fusion, f32[384]{0:T(512)S(1)} %get-tuple-element.47), channel_id=1, replica_groups=mesh['space'=64,'ens'=8] {'space','ens'}, use_global_device_ids=true, to_apply=%region_10.11 | all-reduce | flops 1920 | bytes 15360 | tf_op jit(solution)/shard_map/psum | solution.py:156
  177.6 1.8 fusion.28
  179.4 152.3 %all-reduce.4.cloned.1.call-done = (f32[384,768]{1,0:T(8,128)}, f32[768,384]{1,0:T(8,128)}) async-done(((f32[384,768]{1,0:T(8,128)}, f32[768,384]{1,0:T(8,128)}), (f32[384,768]{1,0:T(8,128)}, f32[768,384]{1,0:T(8,128)})) %all-reduce.4.cloned.1.call-update) | async-done | bytes 2359312 | tf_op jit(solution)/shard_map/psum | solution.py:156
  331.7 2.3 multiply_convert_fusion.1
  (89 shorter events, 15.3 us)
Async XLA Ops:
  7.2 34.4 %copy-start = (bf16[384,768]{1,0:T(8,128)(2,1)S(1)}, bf16[384,768]{1,0:T(8,128)(2,1)}, u32[]{:S(2)}) copy-start(bf16[384,768]{1,0:T(8,128)(2,1)} %param.22) | copy-start | bytes 1769476
  7.2 23.8 %copy-start.12 = (bf16[1,16,16,384]{3,2,1,0:T(8,128)(2,1)S(1)}, bf16[1,16,16,384]{3,2,1,0:T(8,128)(2,1)}, u32[]{:S(2)}) copy-start(bf16[1,16,16,384]{3,2,1,0:T(8,128)(2,1)} %param.17) | copy-start | bytes 589828
  7.2 23.8 %copy-start.15 = (bf16[768,384]{1,0:T(8,128)(2,1)S(1)}, bf16[768,384]{1,0:T(8,128)(2,1)}, u32[]{:S(2)}) copy-start(bf16[768,384]{1,0:T(8,128)(2,1)} %param.23) | copy-start | bytes 1769476
  7.2 324.5 %all-reduce.4.cloned.1.call-start = ((), (), s32[]{:S(2)}) async-start(), calls=%async_computation | async-start | bytes 4718592 | tf_op jit(solution)/shard_map/psum | solution.py:156
  7.2 25.0 %collective-permute-start.1 = (bf16[16,16,384]{2,1,0:T(8,128)(2,1)}, bf16[16,16,384]{2,1,0:T(8,128)(2,1)S(1)}, u32[]{:S(2)}, u32[]{:S(2)}) collective-permute-start(bf16[16,16,384]{2,1,0:T(8,128)(2,1)} %bitcast.100), channel_id=1, source_target_pairs={{8,0},{16,8},{24,16},{32,24},{40,32},{48,40},{56,48},{64,56},{72,6... | collective-permute-start | bytes 589832 | tf_op jit(solution)/shard_map/ppermute | solution.py:24
  22.1 11.8 %collective-permute-start = (bf16[16,16,384]{2,1,0:T(8,128)(2,1)}, bf16[16,16,384]{2,1,0:T(8,128)(2,1)S(1)}, u32[]{:S(2)}, u32[]{:S(2)}) collective-permute-start(bf16[16,16,384]{2,1,0:T(8,128)(2,1)} %bitcast.101), channel_id=1, source_target_pairs={{0,8},{8,16},{16,24},{24,32},{32,40},{40,48},{48,56},{56,64},{64,7... | collective-permute-start | bytes 589832 | tf_op jit(solution)/shard_map/ppermute | solution.py:22
  30.9 1.4 copy-start.19
  30.9 3.0 copy-start.16
  31.0 18.3 %copy-start.9 = (bf16[16,4,16,48]{3,2,0,1:T(8,128)(2,1)}, bf16[16,4,16,48]{3,2,0,1:T(8,128)(2,1)S(1)}, u32[]{:S(2)}) copy-start(bf16[16,4,16,48]{3,2,0,1:T(8,128)(2,1)S(1)} %select_bitcast_fusion) | copy-start | bytes 294916
  38.2 1.7 copy-start.8
  39.9 0.9 copy-start.2
  40.2 0.7 copy-start.4
  40.6 0.8 copy-start.6
  40.6 0.8 copy-start.18
  44.0 1.4 copy-start.13
  58.8 5.3 %copy-start.1 = (f32[17,48,384]{2,1,0:T(8,128)}, f32[17,48,384]{2,1,0:T(8,128)S(1)}, u32[]{:S(2)}) copy-start(f32[17,48,384]{2,1,0:T(8,128)S(1)} %scatter_fusion.2) | copy-start | bytes 3760132
  66.9 12.9 %copy-start.3 = (f32[1,16,16,384]{3,2,1,0:T(8,128)S(1)}, f32[1,16,16,384]{3,2,1,0:T(8,128)}, u32[]{:S(2)}) copy-start(f32[1,16,16,384]{3,2,1,0:T(8,128)} %copy-done.2) | copy-start | bytes 1179652
  66.9 12.9 %copy-start.5 = (f32[1,16,16,384]{3,2,1,0:T(8,128)S(1)}, f32[1,16,16,384]{3,2,1,0:T(8,128)}, u32[]{:S(2)}) copy-start(f32[1,16,16,384]{3,2,1,0:T(8,128)} %copy-done.4) | copy-start | bytes 1179652
  67.0 12.9 %copy-start.7 = (f32[1,16,16,384]{3,2,1,0:T(8,128)S(1)}, f32[1,16,16,384]{3,2,1,0:T(8,128)}, u32[]{:S(2)}) copy-start(f32[1,16,16,384]{3,2,1,0:T(8,128)} %copy-done.6) | copy-start | bytes 1179652
  67.0 12.9 %copy-start.10 = (f32[256,384]{1,0:T(8,128)S(1)}, f32[256,384]{1,0:T(8,128)}, u32[]{:S(2)}) copy-start(f32[256,384]{1,0:T(8,128)} %get-tuple-element.61) | copy-start | bytes 1179652
  70.2 107.4 %copy-start.14 = (bf16[1,16,16,384]{3,2,1,0:T(8,128)(2,1)S(1)}, bf16[1,16,16,384]{3,2,1,0:T(8,128)(2,1)}, u32[]{:S(2)}) copy-start(bf16[1,16,16,384]{3,2,1,0:T(8,128)(2,1)} %param.17) | copy-start | bytes 589828
  70.2 107.4 %collective-permute-start.2 = (bf16[16,16,384]{2,1,0:T(8,128)(2,1)S(1)}, bf16[16,16,384]{2,1,0:T(8,128)(2,1)S(1)}, u32[]{:S(2)}, u32[]{:S(2)}) collective-permute-start(bf16[16,16,384]{2,1,0:T(8,128)(2,1)S(1)} %get-tuple-element.62), channel_id=1, source_target_pairs={{0,8},{8,16},{16,24},{24,32},{32,40},{40,48},{48,56},{56,64},{64,7... | collective-permute-start | bytes 589832 | tf_op jit(solution)/shard_map/ppermute | solution.py:33
  72.3 105.3 %collective-permute-start.3 = (bf16[16,16,384]{2,1,0:T(8,128)(2,1)S(1)}, bf16[16,16,384]{2,1,0:T(8,128)(2,1)S(1)}, u32[]{:S(2)}, u32[]{:S(2)}) collective-permute-start(bf16[16,16,384]{2,1,0:T(8,128)(2,1)S(1)} %get-tuple-element.63), channel_id=1, source_target_pairs={{0,504},{8,0},{16,8},{24,16},{32,24},{40,32},{48,40},{56,48},{64,5... | collective-permute-start | bytes 589832 | tf_op jit(solution)/shard_map/ppermute | solution.py:33
  331.7 2.3 copy-start.11
  (1 other events, 0.7 us)
Sparse Core Ops, SparseCore 0:
  54.3 277.3 all-reduce.3
where the time goes:
time: 342 us
  waiting for transfers between devices  154 us (45%)
  blocking collectives  96.4 us (28%)
  starting transfers between devices  26.4 us (8%)
  other arithmetic  24.5 us (7%)
  matrix products  15.1 us (4%)
  between operations  14.5 us (4%)
  local copies, waits for them, and re-layouts  10.9 us (3%)
    psum x1, waiting for transfers between devices, on_device(): lax.psum((conv_term, gain_term, in_term, out_term), ('space', 'ens'))  152 us
    psum x1, blocking collectives, on_device(): lax.psum((conv_term, gain_term, in_term, out_term), ('space', 'ens'))  96.4 us
    ppermute x1, starting transfers between devices, padded(): lax.ppermute(head, axis, [((i + 1) % count, i) for i in range(count)])  14.8 us
    scatter-add x4, other arithmetic, sum_rows(): jax.ops.segment_sum(values, targets, num_segments=row_count + 1)[:row_count]  11.2 us
    ppermute x2, starting transfers between devices, from_behind(): lax.ppermute(value, axis, [(i, (i + by) % peers) for i in range(peers)])  9.63 us
  transfers between devices with their start and end apart: 5, of which 2 were waited for; matrix products, arithmetic and copies ran while one was open for 8% of the time, Pallas kernels for 0%

commit v1 on v0

v1 whole, which is shorter than its diff:
```python
import math

import jax
import jax.numpy as jnp
from jax import lax
from jax.sharding import Mesh, PartitionSpec as P

K = 4
HMAX = 16
REACH = 2
SPAN = 2 * REACH + 1
EXTRA = 8


norm_eps = 1e-05
f32 = jnp.float32
bf16 = jnp.bfloat16
SPACE = ("x", "z", "yl")
ENS = ("yh", "core")


def shifted(value, axes, by):
    count = lax.axis_size(axes)
    return lax.ppermute(value, axes, [(i, (i + by) % count) for i in range(count)])


def swap_cores(value):
    return lax.ppermute(value, "core", [(0, 1), (1, 0)])


def band_blocks(halo_cols, row_offset, row_count, col_count):
    padded = col_count + 2 * HMAX
    shape = (row_count, K * col_count, SPAN * padded)
    out_id = lax.broadcasted_iota(jnp.int32, shape, 1)
    src_id = lax.broadcasted_iota(jnp.int32, shape, 2)
    basis = out_id // col_count
    column = out_id % col_count
    source_row = src_id // padded - REACH
    step = src_id % padded - column - HMAX
    reach = halo_cols[:, None, None]
    ratio = step.astype(f32) / (reach.astype(f32) + 1.0)
    square = ratio * ratio
    power = jnp.where(basis == 0, 1.0, jnp.where(basis == 1, ratio, jnp.where(basis == 2, square, ratio * square)))
    value = (1.0 - square) / jnp.sqrt(reach.astype(f32) + 1.0) * power
    chosen = jnp.repeat(row_offset, col_count, axis=1)[:, :, None] == source_row
    inside = (jnp.abs(step) <= reach) & chosen
    return jnp.where(inside, value, 0.0).astype(bf16)


def split_pair(value):
    high = lax.reduce_precision(value, 8, 7)
    low = lax.reduce_precision(value - high, 8, 7)
    return high, low


def exchange(blocks, axes):
    return lax.all_to_all(blocks, axes, 0, 0, tiled=True)


def with_extras(blocks, extras):
    high, low = split_pair(extras)
    pair = jnp.concatenate([high, low], axis=0).astype(bf16)
    wide = jnp.broadcast_to(pair[None], (blocks.shape[0],) + pair.shape)
    return jnp.concatenate([blocks, wide], axis=1)


def summed(received, rows):
    total = jnp.sum(received.astype(f32), axis=0)
    return total[:rows], total[rows : rows + EXTRA] + total[rows + EXTRA :]


def reduce_all(in_term, out_term, extras, factor):
    core = lax.axis_index("core")
    rows, channels = in_term.shape
    mine = jnp.where(core == 0, in_term, out_term)
    theirs = jnp.where(core == 0, out_term, in_term).astype(bf16)
    high, low = split_pair(extras)
    got = swap_cores(jnp.concatenate([theirs, high.astype(bf16), low.astype(bf16)], axis=0)).astype(f32)
    mine = mine + got[:rows]
    extras = (high + low) + (got[rows : rows + EXTRA] + got[rows + EXTRA :])
    for axes in (("x", "yl"), ("yh",)):
        count = lax.axis_size(axes)
        rows = rows // count
        blocks = mine.astype(bf16).reshape(count, rows, channels)
        mine, extras = summed(exchange(with_extras(blocks, extras), axes), rows)
    count = lax.axis_size("z")
    blocks = jnp.broadcast_to(mine.astype(bf16)[None], (count, rows, channels))
    mine, extras = summed(exchange(with_extras(blocks, extras), "z"), rows)
    mine = (mine * factor).astype(bf16)
    for axes in (("yh",), ("x", "yl")):
        count = lax.axis_size(axes)
        blocks = jnp.broadcast_to(mine[None], (count, rows, channels))
        rows = rows * count
        mine = exchange(blocks, axes).reshape(rows, channels)
    other = swap_cores(mine)
    return jnp.where(core == 0, mine, other), jnp.where(core == 0, other, mine), extras * factor


def contract_cells(left, right):
    return lax.dot_general(left, right, (((0,), (0,)), ((), ())), preferred_element_type=f32)


def contract_features(left, right):
    return lax.dot_general(left, right, (((1,), (1,)), ((), ())), preferred_element_type=f32)


def on_device(state, cotangent, halo_cols, row_offset, conv_weight, norm_gain, weight_in, weight_out):
    local_state = state[0]
    local_grad = cotangent[0]
    row_count, col_count, channels = local_state.shape
    padded = col_count + 2 * HMAX
    west = shifted(local_state[:, col_count - HMAX :], SPACE, 1)
    east = shifted(local_state[:, :HMAX], SPACE, -1)
    bands = band_blocks(halo_cols, row_offset, row_count, col_count)
    extended = jnp.pad(
        jnp.concatenate([west, local_state, east], axis=1), ((REACH, REACH), (0, 0), (0, 0))
    )
    windows = jnp.stack(
        [extended[r : r + SPAN].reshape(SPAN * padded, channels) for r in range(row_count)]
    )
    responses = jnp.einsum("rmw,rwc->rmc", bands, windows, preferred_element_type=f32)
    responses = responses.reshape(row_count, K, col_count, channels)
    filtered = jnp.sum(conv_weight[None, :, None, :] * responses, axis=1)
    cell_count = row_count * col_count
    flat_mixed = filtered.reshape(cell_count, channels)
    center = jnp.mean(flat_mixed, axis=-1, keepdims=True)
    offset_vals = flat_mixed - center
    variance = jnp.mean(offset_vals * offset_vals, axis=-1, keepdims=True)
    inverse = 1.0 / jnp.sqrt(variance + norm_eps)
    normed = offset_vals * inverse
    scaled = (normed * norm_gain).astype(bf16)
    preact = jnp.dot(scaled, weight_in, preferred_element_type=f32)
    hidden_vals, gelu_back = jax.vjp(jax.nn.gelu, preact)
    hidden = hidden_vals.astype(bf16)
    flat_grad = local_grad.reshape(cell_count, channels)
    factor = 1.0 / math.sqrt(lax.axis_size(ENS) * cell_count * lax.axis_size(SPACE))
    out_term = contract_cells(hidden, flat_grad)
    grad_hidden = contract_features(flat_grad, weight_out)
    grad_preact = gelu_back(grad_hidden)[0].astype(bf16)
    half = grad_preact.shape[1] // 2
    in_term = jnp.concatenate(
        [contract_cells(scaled, grad_preact[:, :half]), contract_cells(scaled, grad_preact[:, half:])], axis=0
    )
    grad_scaled = contract_features(grad_preact, weight_in)
    gain_term = jnp.sum(grad_scaled * normed, axis=0)
    grad_normed = grad_scaled * norm_gain
    grad_filtered = (
        grad_normed
        - jnp.mean(grad_normed, axis=-1, keepdims=True)
        - normed * jnp.mean(grad_normed * normed, axis=-1, keepdims=True)
    ) * inverse
    grad_field = grad_filtered.reshape(row_count, col_count, channels)
    conv_term = jnp.sum(grad_field[:, None] * responses, axis=(0, 2))
    grad_rounded = grad_field.astype(bf16).astype(f32)
    weighted = (conv_weight[None, :, None, :] * grad_rounded[:, None]).astype(bf16)
    weighted = weighted.reshape(row_count, K * col_count, channels)
    parts = jnp.einsum("rmw,rmc->rwc", bands, weighted, preferred_element_type=f32)
    parts = parts.reshape(row_count, SPAN, padded, channels)
    spread_out = jnp.zeros((row_count, padded, channels), f32)
    for at in range(SPAN):
        by = at - REACH
        low, high = max(0, -by), row_count - max(0, by)
        spread_out = spread_out + jnp.pad(
            parts[low:high, at], ((max(0, by), max(0, -by)), (0, 0), (0, 0))
        )
    from_east = shifted(spread_out[:, :HMAX].astype(bf16), SPACE, -1).astype(f32)
    from_west = shifted(spread_out[:, col_count + HMAX :].astype(bf16), SPACE, 1).astype(f32)
    interior = spread_out[:, HMAX : HMAX + col_count]
    interior = interior.at[:, :HMAX].add(from_west)
    interior = interior.at[:, col_count - HMAX :].add(from_east)
    grad_state = (local_grad.astype(f32) + interior).astype(bf16)[None]
    extras = jnp.concatenate(
        [conv_term, gain_term[None], jnp.zeros((EXTRA - K - 1, channels), f32)], axis=0
    )
    in_total, grad_out, extra_total = reduce_all(in_term, out_term, extras, factor)
    grad_in = jnp.concatenate([in_total[:channels], in_total[channels:]], axis=1)
    return (grad_state, extra_total[:K], extra_total[K], grad_in, grad_out)


def solution(mesh):
    fine = Mesh(mesh.devices.reshape(4, 8, 2, 4, 2), SPACE + ENS)
    field = P(ENS, None, SPACE, None)
    return jax.shard_map(
        on_device,
        mesh=fine,
        in_specs=(field, field, P(), P(), P(), P(), P(), P()),
        out_specs=(field, P(), P(), P(), P()),
        check_vma=False,
    )
```

time: 342 us -> 124 us (0.36)
  waiting for transfers between devices: 154 us -> 26.5 us
  blocking collectives: 96.4 us -> 13.8 us
  starting transfers between devices: 26.4 us -> 54.2 us
  other arithmetic: 24.5 us -> 9.7 us
  between operations: 14.5 us -> 1.27 us
  matrix products: 15.1 us -> 8.77 us
    psum x1 -> x0, waiting for transfers between devices: 152 us -> none  [on_device(): lax.psum((conv_term, gain_term, in_term, out_term), ('space', 'ens'))]
    psum x1 -> x0, blocking collectives: 96.4 us -> none  [on_device(): lax.psum((conv_term, gain_term, in_term, out_term), ('space', 'ens'))]
    all_to_all x0 -> x4, waiting for transfers between devices: none -> 17.7 us  [exchange(): return lax.all_to_all(blocks, axes, 0, 0, tiled=True)]
    all_to_all x0 -> x4, starting transfers between devices: none -> 16.2 us  [exchange(): return lax.all_to_all(blocks, axes, 0, 0, tiled=True)]
    all_to_all x0 -> x1, blocking collectives: none -> 13.8 us  [exchange(): return lax.all_to_all(blocks, axes, 0, 0, tiled=True)]
    ppermute x4 -> x6, starting transfers between devices: 26.4 us -> 38 us  [the longest x4 26.3 us: shifted(): lax.ppermute(value, axes, [(i, (i + by) % count) for i in range(count)])]
    scatter-add x4 -> x0, other arithmetic: 11.2 us -> none  [sum_rows(): jax.ops.segment_sum(values, targets, num_segments=row_count + 1)[:row_count]]
    gather x6 -> x0, local copies, waits for them, and re-layouts: 7.67 us -> none  [the longest x4 4.23 us: pick_rows(): picked = values[jnp.clip(source, 0, row_count - 1)]]
  transfers between devices with their start and end apart: 5 -> 10, of which waited for: 2 -> 5; matrix products, arithmetic and copies ran while one was open for 8% -> 13% of each run, Pallas kernels for 0% -> 0%
where the time goes in v1:
time: 124 us; the launch traced here: 123 us
  starting transfers between devices  54.2 us (44%)
  waiting for transfers between devices  26.5 us (21%)
  blocking collectives  13.8 us (11%)
  other arithmetic  9.7 us (8%)
  local copies, waits for them, and re-layouts  9.16 us (7%)
  matrix products  8.77 us (7%)
  between operations  1.27 us (1%)
    ppermute x4, starting transfers between devices, shifted(): lax.ppermute(value, axes, [(i, (i + by) % count) for i in range(count)])  26.3 us
    all_to_all x4, waiting for transfers between devices, exchange(): return lax.all_to_all(blocks, axes, 0, 0, tiled=True)  17.7 us
    all_to_all x4, starting transfers between devices, exchange(): return lax.all_to_all(blocks, axes, 0, 0, tiled=True)  16.2 us
    all_to_all x1, blocking collectives, exchange(): return lax.all_to_all(blocks, axes, 0, 0, tiled=True)  13.8 us
    ppermute x2, starting transfers between devices, swap_cores(): return lax.ppermute(value, 'core', [(0, 1), (1, 0)])  11.8 us
    ppermute x4, waiting for transfers between devices, shifted(): lax.ppermute(value, axes, [(i, (i + by) % count) for i in range(count)])  7.17 us
    dot_general x1, matrix products, on_device(): jnp.einsum('rmw,rmc->rwc', bands, weighted, preferred_element_type=f32)  3.73 us
    squeeze x2, local copies, waits for them, and re-layouts, on_device(): parts[low:high, at]  3.4 us
  transfers between devices with their start and end apart: 10, of which 5 were waited for; matrix products, arithmetic and copies ran while one was open for 13% of the time, Pallas kernels for 0%

profile of v1, /device:TPU:1, one launch (start us, length us, event | category | flops | bytes accessed | tf_op | source)
XLA Modules:
  0.0 123.4 jit_solution(8119457495470098746)
XLA Ops:
  0.7 14.8 %collective-permute-start.1 = (bf16[16,16,384]{2,1,0:T(8,128)(2,1)}, bf16[16,16,384]{2,1,0:T(8,128)(2,1)S(1)}, u32[]{:S(2)}, u32[]{:S(2)}) collective-permute-start(bf16[16,16,384]{2,1,0:T(8,128)(2,1)} %bitcast.156), channel_id=1, source_target_pairs={{0,504},{8,0},{16,8},{24,16},{32,24},{40,32},{48,40},{56,48},{64,5... | collective-permute-start | bytes 589832 | tf_op jit(solution)/shard_map/ppermute | solution.py:24
  15.5 1.9 %collective-permute-start = (bf16[16,16,384]{2,1,0:T(8,128)(2,1)}, bf16[16,16,384]{2,1,0:T(8,128)(2,1)S(1)}, u32[]{:S(2)}, u32[]{:S(2)}) collective-permute-start(bf16[16,16,384]{2,1,0:T(8,128)(2,1)} %bitcast.157), channel_id=1, source_target_pairs={{0,8},{8,16},{16,24},{24,32},{32,40},{40,48},{48,56},{56,64},{64,7... | collective-permute-start | bytes 589832 | tf_op jit(solution)/shard_map/ppermute | solution.py:24
  18.5 1.6 %fusion.61 = f32[256,768]{1,0:T(8,128)S(1)} fusion(bf16[256,384]{1,0:T(8,128)(2,1)} %bitcast.133, bf16[768,384]{1,0:T(8,128)(2,1)} %param.23), kind=kOutput, calls=%fused_computation.160 | convolution fusion | flops 150994944 | bytes 1572864 | tf_op jit(solution)/shard_map/dot_general | solution.py:104
  20.1 7.2 %collective-permute-done = bf16[16,16,384]{2,1,0:T(8,128)(2,1)S(1)} collective-permute-done((bf16[16,16,384]{2,1,0:T(8,128)(2,1)}, bf16[16,16,384]{2,1,0:T(8,128)(2,1)S(1)}, u32[]{:S(2)}, u32[]{:S(2)}) %collective-permute-start) | collective-permute-done | bytes 196640 | tf_op jit(solution)/shard_map/ppermute | solution.py:24
  28.6 1.2 multiply_reduce_fusion
  34.0 3.8 %collective-permute-start.4 = (bf16[784,384]{1,0:T(8,128)(2,1)S(1)}, bf16[784,384]{1,0:T(8,128)(2,1)S(1)}, u32[]{:S(2)}, u32[]{:S(2)}) collective-permute-start(bf16[784,384]{1,0:T(8,128)(2,1)S(1)} %pad_maximum_fusion.2), channel_id=1, source_target_pairs={{0,1},{1,0},{2,3},{3,2},{4,5},{5,4},{6,7},{7,6},{8,9},{9,8},{10,11... | collective-permute-start | bytes 1806344 | tf_op jit(solution)/shard_map/ppermute | solution.py:28
  37.8 1.6 %collective-permute-done.4 = bf16[784,384]{1,0:T(8,128)(2,1)S(1)} collective-permute-done((bf16[784,384]{1,0:T(8,128)(2,1)S(1)}, bf16[784,384]{1,0:T(8,128)(2,1)S(1)}, u32[]{:S(2)}, u32[]{:S(2)}) %collective-permute-start.4) | collective-permute-done | bytes 602144 | tf_op jit(solution)/shard_map/ppermute | solution.py:28
  39.9 13.8 %all_to_all.25 = bf16[8,112,384]{2,1,0:T(8,128)(2,1)S(1)} all-to-all(bf16[8,112,384]{2,1,0:T(8,128)(2,1)S(1)} %pad_maximum_fusion.1), channel_id=1, replica_groups=mesh['x'=4,'z'=8,'yl'=2,'yh'=4,'core'=2] {'x','yl'}, dimensions={0} | all-to-all | bytes 1376256 | tf_op jit(solution)/shard_map/all_to_all | solution.py:57
  54.6 5.9 %all-to-all-start.1 = ((bf16[4,40,384]{2,1,0:T(8,128)(2,1)}), bf16[4,40,384]{2,1,0:T(8,128)(2,1)S(1)}, u32[]{:S(2)}, u32[]{:S(2)}) async-start(bf16[4,40,384]{2,1,0:T(8,128)(2,1)} %pad_maximum_fusion.6), calls=%async_computation.1 | async-start | bytes 245760 | tf_op jit(solution)/shard_map/all_to_all | solution.py:57
  60.7 7.0 %all-to-all-done.1 = bf16[4,40,384]{2,1,0:T(8,128)(2,1)S(1)} async-done(((bf16[4,40,384]{2,1,0:T(8,128)(2,1)}), bf16[4,40,384]{2,1,0:T(8,128)(2,1)S(1)}, u32[]{:S(2)}, u32[]{:S(2)}) %all-to-all-start.1) | async-done | bytes 122912 | tf_op jit(solution)/shard_map/all_to_all | solution.py:57
  68.5 3.4 %all-to-all-start.2 = ((bf16[8,40,384]{2,1,0:T(8,128)(2,1)}), bf16[8,40,384]{2,1,0:T(8,128)(2,1)S(1)}, u32[]{:S(2)}, u32[]{:S(2)}) async-start(bf16[8,40,384]{2,1,0:T(8,128)(2,1)} %pad_maximum_fusion.5), calls=%async_computation.2 | async-start | bytes 491520 | tf_op jit(solution)/shard_map/all_to_all | solution.py:57
  72.0 3.7 %fusion.52 = f32[16,240,384]{2,1,0:T(8,128)} fusion(bf16[16,64,384]{2,1,0:T(8,128)(2,1)S(1)} %fusion.1, s32[64]{0:T(128)S(1)} %get-tuple-element.103, s32[64]{0:T(128)S(1)} %get-tuple-element.105, f32[16]{0:T(128)S(1)} %get-tuple-element.87, f32[16]{0:T(128)S(1)} %get-tuple-element.86, s32[240]{0:T(256)S(1)} %get-tuple-element.99, ...), kind=kOutput, calls=%fused_computation.155 | convolution fusion | flops 195133440 | bytes 6694432 | tf_op jit(solution)/shard_map/rmw,rmc->rwc/dot_general | solution.py:157
  75.7 5.4 %all-to-all-done.2 = bf16[8,40,384]{2,1,0:T(8,128)(2,1)S(1)} async-done(((bf16[8,40,384]{2,1,0:T(8,128)(2,1)}), bf16[8,40,384]{2,1,0:T(8,128)(2,1)S(1)}, u32[]{:S(2)}, u32[]{:S(2)}) %all-to-all-start.2) | async-done | bytes 245792 | tf_op jit(solution)/shard_map/all_to_all | solution.py:57
  81.8 3.3 %all-to-all-start.3 = ((bf16[4,24,384]{2,1,0:T(8,128)(2,1)}), bf16[4,24,384]{2,1,0:T(8,128)(2,1)S(1)}, u32[]{:S(2)}, u32[]{:S(2)}) async-start(bf16[4,24,384]{2,1,0:T(8,128)(2,1)} %broadcast_in_dim.37), calls=%async_computation.3 | async-start | bytes 147456 | tf_op jit(solution)/shard_map/all_to_all | solution.py:57
  85.1 1.7 %slice_bitcast_fusion.2 = (f32[15,48,384]{2,1,0:T(8,128)S(1)}, f32[15,48,384]{2,1,0:T(8,128)S(1)}) fusion(f32[16,5,48,384]{3,2,1,0:T(8,128)} %bitcast.128), kind=kLoop, calls=%fused_computation.24 | loop fusion | bytes 4423680 | tf_op jit(solution)/shard_map/squeeze | solution.py:164
  86.9 5.2 %all-to-all-done.3 = bf16[4,24,384]{2,1,0:T(8,128)(2,1)S(1)} async-done(((bf16[4,24,384]{2,1,0:T(8,128)(2,1)}), bf16[4,24,384]{2,1,0:T(8,128)(2,1)S(1)}, u32[]{:S(2)}, u32[]{:S(2)}) %all-to-all-start.3) | async-done | bytes 73760 | tf_op jit(solution)/shard_map/all_to_all | solution.py:57
  92.9 3.5 %all-to-all-start.4 = ((bf16[8,96,384]{2,1,0:T(8,128)(2,1)}), bf16[8,96,384]{2,1,0:T(8,128)(2,1)S(1)}, u32[]{:S(2)}, u32[]{:S(2)}) async-start(bf16[8,96,384]{2,1,0:T(8,128)(2,1)} %broadcast_in_dim.39), calls=%async_computation.4 | async-start | bytes 1179648 | tf_op jit(solution)/shard_map/all_to_all | solution.py:57
  96.4 1.7 %slice_bitcast_fusion.4 = (f32[14,48,384]{2,1,0:T(8,128)S(1)}, f32[14,48,384]{2,1,0:T(8,128)S(1)}) fusion(f32[16,5,48,384]{3,2,1,0:T(8,128)} %bitcast.129), kind=kLoop, calls=%fused_computation.35 | loop fusion | bytes 4128768 | tf_op jit(solution)/shard_map/squeeze | solution.py:164
  98.1 2.7 %fusion.57 = (bf16[16,48,384]{2,1,0:T(8,128)(2,1)S(1)}, f32[16,48,384]{2,1,0:T(8,128)}) fusion(f32[14,48,384]{2,1,0:T(8,128)S(1)} %get-tuple-element.55, f32[15,48,384]{2,1,0:T(8,128)S(1)} %get-tuple-element.57, f32[16,5,48,384]{3,2,1,0:T(8,128)} %bitcast.130, f32[15,48,384]{2,1,0:T(8,128)S(1)} %get-tuple-element.56, f32[14,48,384]{2,1,0:T(8,128)S(1)} %get-tuple-element.54), kind=kLoop, calls=%fused_computation.157 | loop fusion | flops 1474560 | bytes 7225344 | tf_op jit(solution)/shard_map/convert.10
  100.9 3.3 %collective-permute-start.2 = (bf16[16,16,384]{2,1,0:T(8,128)(2,1)S(1)}, bf16[16,16,384]{2,1,0:T(8,128)(2,1)S(1)}, u32[]{:S(2)}, u32[]{:S(2)}) collective-permute-start(bf16[16,16,384]{2,1,0:T(8,128)(2,1)S(1)} %get-tuple-element.62), channel_id=1, source_target_pairs={{0,8},{8,16},{16,24},{24,32},{32,40},{40,48},{48,56},{56,64},{64,7... | collective-permute-start | bytes 589832 | tf_op jit(solution)/shard_map/ppermute | solution.py:24
  104.2 6.2 %collective-permute-start.3 = (bf16[16,16,384]{2,1,0:T(8,128)(2,1)S(1)}, bf16[16,16,384]{2,1,0:T(8,128)(2,1)S(1)}, u32[]{:S(2)}, u32[]{:S(2)}) collective-permute-start(bf16[16,16,384]{2,1,0:T(8,128)(2,1)S(1)} %get-tuple-element.63), channel_id=1, source_target_pairs={{0,504},{8,0},{16,8},{24,16},{32,24},{40,32},{48,40},{56,48},{64,5... | collective-permute-start | bytes 589832 | tf_op jit(solution)/shard_map/ppermute | solution.py:24
  110.4 8.0 %collective-permute-start.5 = (bf16[768,384]{1,0:T(8,128)(2,1)S(1)}, bf16[768,384]{1,0:T(8,128)(2,1)S(1)}, u32[]{:S(2)}, u32[]{:S(2)}) collective-permute-start(bf16[768,384]{1,0:T(8,128)(2,1)S(1)} %bitcast.132), channel_id=1, source_target_pairs={{0,1},{1,0},{2,3},{3,2},{4,5},{5,4},{6,7},{7,6},{8,9},{9,8},{10,11... | collective-permute-start | bytes 1769480 | tf_op jit(solution)/shard_map/ppermute | solution.py:28
  118.5 1.8 %fusion.29 = bf16[1,16,16,384]{3,2,1,0:T(8,128)(2,1)} fusion(bf16[16,16,384]{2,1,0:T(8,128)(2,1)S(1)} %collective-permute-done.3, bf16[16,16,384]{2,1,0:T(8,128)(2,1)S(1)} %collective-permute-done.2, f32[16,48,384]{2,1,0:T(8,128)} %get-tuple-element.51, bf16[1,16,16,384]{3,2,1,0:T(8,128)(2,1)} %param.17), kind=kLoop, calls=%fused_computation.74 | loop fusion | flops 688128 | bytes 1179648 | tf_op jit(solution)/shard_map/broadcast_in_dim | solution.py:171
  121.5 1.0 broadcast_select_fusion
  (101 shorter events, 12.2 us)
Async XLA Ops:
  0.6 30.0 %copy-start = (bf16[384,768]{1,0:T(8,128)(2,1)S(1)}, bf16[384,768]{1,0:T(8,128)(2,1)}, u32[]{:S(2)}) copy-start(bf16[384,768]{1,0:T(8,128)(2,1)} %param.22) | copy-start | bytes 1769476
  0.6 26.6 %copy-start.2 = (bf16[1,16,16,384]{3,2,1,0:T(8,128)(2,1)S(1)}, bf16[1,16,16,384]{3,2,1,0:T(8,128)(2,1)}, u32[]{:S(2)}) copy-start(bf16[1,16,16,384]{3,2,1,0:T(8,128)(2,1)} %param.16) | copy-start | bytes 589828
  0.7 19.4 %copy-start.5 = (s32[16]{0:T(128)S(1)}, s32[16]{0:T(128)}, u32[]{:S(2)}) copy-start(s32[16]{0:T(128)} %param.18) | copy-start | bytes 196
  0.7 19.4 %collective-permute-start.1 = (bf16[16,16,384]{2,1,0:T(8,128)(2,1)}, bf16[16,16,384]{2,1,0:T(8,128)(2,1)S(1)}, u32[]{:S(2)}, u32[]{:S(2)}) collective-permute-start(bf16[16,16,384]{2,1,0:T(8,128)(2,1)} %bitcast.156), channel_id=1, source_target_pairs={{0,504},{8,0},{16,8},{24,16},{32,24},{40,32},{48,40},{56,48},{64,5... | collective-permute-start | bytes 589832 | tf_op jit(solution)/shard_map/ppermute | solution.py:24
  15.5 11.8 %collective-permute-start = (bf16[16,16,384]{2,1,0:T(8,128)(2,1)}, bf16[16,16,384]{2,1,0:T(8,128)(2,1)S(1)}, u32[]{:S(2)}, u32[]{:S(2)}) collective-permute-start(bf16[16,16,384]{2,1,0:T(8,128)(2,1)} %bitcast.157), channel_id=1, source_target_pairs={{0,8},{8,16},{16,24},{24,32},{32,40},{40,48},{48,56},{56,64},{64,7... | collective-permute-start | bytes 589832 | tf_op jit(solution)/shard_map/ppermute | solution.py:24
  27.9 0.7 copy-start.3
  29.8 0.7 copy-start.4
  32.5 0.9 copy-start.1
  34.0 5.4 %collective-permute-start.4 = (bf16[784,384]{1,0:T(8,128)(2,1)S(1)}, bf16[784,384]{1,0:T(8,128)(2,1)S(1)}, u32[]{:S(2)}, u32[]{:S(2)}) collective-permute-start(bf16[784,384]{1,0:T(8,128)(2,1)S(1)} %pad_maximum_fusion.2), channel_id=1, source_target_pairs={{0,1},{1,0},{2,3},{3,2},{4,5},{5,4},{6,7},{7,6},{8,9},{9,8},{10,11... | collective-permute-start | bytes 1806344 | tf_op jit(solution)/shard_map/ppermute | solution.py:28
  54.6 13.1 %all-to-all-start.1 = ((bf16[4,40,384]{2,1,0:T(8,128)(2,1)}), bf16[4,40,384]{2,1,0:T(8,128)(2,1)S(1)}, u32[]{:S(2)}, u32[]{:S(2)}) async-start(bf16[4,40,384]{2,1,0:T(8,128)(2,1)} %pad_maximum_fusion.6), calls=%async_computation.1 | async-start | bytes 245760 | tf_op jit(solution)/shard_map/all_to_all | solution.py:57
  68.5 12.6 %all-to-all-start.2 = ((bf16[8,40,384]{2,1,0:T(8,128)(2,1)}), bf16[8,40,384]{2,1,0:T(8,128)(2,1)S(1)}, u32[]{:S(2)}, u32[]{:S(2)}) async-start(bf16[8,40,384]{2,1,0:T(8,128)(2,1)} %pad_maximum_fusion.5), calls=%async_computation.2 | async-start | bytes 491520 | tf_op jit(solution)/shard_map/all_to_all | solution.py:57
  81.8 10.2 %all-to-all-start.3 = ((bf16[4,24,384]{2,1,0:T(8,128)(2,1)}), bf16[4,24,384]{2,1,0:T(8,128)(2,1)S(1)}, u32[]{:S(2)}, u32[]{:S(2)}) async-start(bf16[4,24,384]{2,1,0:T(8,128)(2,1)} %broadcast_in_dim.37), calls=%async_computation.3 | async-start | bytes 147456 | tf_op jit(solution)/shard_map/all_to_all | solution.py:57
  92.9 17.5 %all-to-all-start.4 = ((bf16[8,96,384]{2,1,0:T(8,128)(2,1)}), bf16[8,96,384]{2,1,0:T(8,128)(2,1)S(1)}, u32[]{:S(2)}, u32[]{:S(2)}) async-start(bf16[8,96,384]{2,1,0:T(8,128)(2,1)} %broadcast_in_dim.39), calls=%async_computation.4 | async-start | bytes 1179648 | tf_op jit(solution)/shard_map/all_to_all | solution.py:57
  100.9 17.5 %collective-permute-start.2 = (bf16[16,16,384]{2,1,0:T(8,128)(2,1)S(1)}, bf16[16,16,384]{2,1,0:T(8,128)(2,1)S(1)}, u32[]{:S(2)}, u32[]{:S(2)}) collective-permute-start(bf16[16,16,384]{2,1,0:T(8,128)(2,1)S(1)} %get-tuple-element.62), channel_id=1, source_target_pairs={{0,8},{8,16},{16,24},{24,32},{32,40},{40,48},{48,56},{56,64},{64,7... | collective-permute-start | bytes 589832 | tf_op jit(solution)/shard_map/ppermute | solution.py:24
  104.2 14.3 %collective-permute-start.3 = (bf16[16,16,384]{2,1,0:T(8,128)(2,1)S(1)}, bf16[16,16,384]{2,1,0:T(8,128)(2,1)S(1)}, u32[]{:S(2)}, u32[]{:S(2)}) collective-permute-start(bf16[16,16,384]{2,1,0:T(8,128)(2,1)S(1)} %get-tuple-element.63), channel_id=1, source_target_pairs={{0,504},{8,0},{16,8},{24,16},{32,24},{40,32},{48,40},{56,48},{64,5... | collective-permute-start | bytes 589832 | tf_op jit(solution)/shard_map/ppermute | solution.py:24
  110.4 11.1 %collective-permute-start.5 = (bf16[768,384]{1,0:T(8,128)(2,1)S(1)}, bf16[768,384]{1,0:T(8,128)(2,1)S(1)}, u32[]{:S(2)}, u32[]{:S(2)}) collective-permute-start(bf16[768,384]{1,0:T(8,128)(2,1)S(1)} %bitcast.132), channel_id=1, source_target_pairs={{0,1},{1,0},{2,3},{3,2},{4,5},{5,4},{6,7},{7,6},{8,9},{9,8},{10,11... | collective-permute-start | bytes 1769480 | tf_op jit(solution)/shard_map/ppermute | solution.py:28

commit v2 on v1

--- a/solution.py
+++ b/solution.py
@@ -47,10 +47,8 @@
     return jnp.where(inside, value, 0.0).astype(bf16)
 
 
-def split_pair(value):
-    high = lax.reduce_precision(value, 8, 7)
-    low = lax.reduce_precision(value - high, 8, 7)
-    return high, low
+def rounded(value):
+    return lax.reduce_precision(value, 8, 7)
 
 
 def exchange(blocks, axes):
@@ -58,42 +56,59 @@
 
 
 def with_extras(blocks, extras):
-    high, low = split_pair(extras)
-    pair = jnp.concatenate([high, low], axis=0).astype(bf16)
-    wide = jnp.broadcast_to(pair[None], (blocks.shape[0],) + pair.shape)
+    wide = jnp.broadcast_to(extras.astype(bf16)[None], (blocks.shape[0],) + extras.shape)
     return jnp.concatenate([blocks, wide], axis=1)
 
 
 def summed(received, rows):
     total = jnp.sum(received.astype(f32), axis=0)
-    return total[:rows], total[rows : rows + EXTRA] + total[rows + EXTRA :]
-
-
-def reduce_all(in_term, out_term, extras, factor):
+    return total[:rows], total[rows:]
+
+
+def copies(value, count):
+    return jnp.broadcast_to(value[None], (count,) + value.shape)
+
+
+def reduce_all(in_term, out_term, extras, factor, beside):
+    seed, adjoint, send, finish = beside
     core = lax.axis_index("core")
-    rows, channels = in_term.shape
-    mine = jnp.where(core == 0, in_term, out_term)
-    theirs = jnp.where(core == 0, out_term, in_term).astype(bf16)
-    high, low = split_pair(extras)
-    got = swap_cores(jnp.concatenate([theirs, high.astype(bf16), low.astype(bf16)], axis=0)).astype(f32)
+    channels = extras.shape[1]
+    first = jnp.concatenate([in_term[0], out_term[:channels]], axis=0)
+    second = jnp.concatenate([in_term[1], out_term[channels:]], axis=0)
+    rows = 2 * channels
+    mine = jnp.where(core == 0, first, second)
+    theirs = jnp.where(core == 0, second, first).astype(bf16)
+    extras = rounded(extras)
+    got = swap_cores(jnp.concatenate([theirs, extras.astype(bf16)], axis=0)).astype(f32)
     mine = mine + got[:rows]
-    extras = (high + low) + (got[rows : rows + EXTRA] + got[rows + EXTRA :])
-    for axes in (("x", "yl"), ("yh",)):
-        count = lax.axis_size(axes)
-        rows = rows // count
-        blocks = mine.astype(bf16).reshape(count, rows, channels)
-        mine, extras = summed(exchange(with_extras(blocks, extras), axes), rows)
-    count = lax.axis_size("z")
-    blocks = jnp.broadcast_to(mine.astype(bf16)[None], (count, rows, channels))
-    mine, extras = summed(exchange(with_extras(blocks, extras), "z"), rows)
-    mine = (mine * factor).astype(bf16)
-    for axes in (("yh",), ("x", "yl")):
-        count = lax.axis_size(axes)
-        blocks = jnp.broadcast_to(mine[None], (count, rows, channels))
-        rows = rows * count
-        mine = exchange(blocks, axes).reshape(rows, channels)
+    extras = extras + got[rows:]
+    rows = rows // 8
+    blocks = with_extras(mine.astype(bf16).reshape(8, rows, channels), extras)
+    blocks, seed = lax.optimization_barrier((blocks, seed))
+    work = adjoint(seed)
+    got, work = lax.optimization_barrier((exchange(blocks, ("x", "yl")), work))
+    mine, extras = summed(got, rows)
+    rows = rows // 4
+    blocks = with_extras(mine.astype(bf16).reshape(4, rows, channels), extras)
+    mine, extras = summed(exchange(blocks, ("yh",)), rows)
+    blocks = copies(jnp.concatenate([mine, extras], axis=0).astype(bf16), 8)
+    blocks, edges = lax.optimization_barrier((blocks, work[:2]))
+    sent = send(edges)
+    total = jnp.sum(exchange(blocks, ("z",)).astype(f32), axis=0) * factor
+    blocks = copies(total[:rows].astype(bf16), 4)
+    rows = rows * 4
+    mine = exchange(blocks, ("yh",)).reshape(rows, channels)
+    blocks, sent = lax.optimization_barrier((copies(mine, 8), sent))
+    rows = rows * 8
+    mine = exchange(blocks, ("x", "yl")).reshape(rows, channels)
+    mine, sent, work, total = lax.optimization_barrier((mine, sent, work, total))
     other = swap_cores(mine)
-    return jnp.where(core == 0, mine, other), jnp.where(core == 0, other, mine), extras * factor
+    done = finish(work, sent)
+    first = jnp.where(core == 0, mine, other)
+    second = jnp.where(core == 0, other, mine)
+    grad_in = jnp.concatenate([first[:channels], second[:channels]], axis=1)
+    grad_out = jnp.concatenate([first[channels:], second[channels:]], axis=0)
+    return grad_in, grad_out, total[total.shape[0] - EXTRA :], done
 
 
 def contract_cells(left, right):
@@ -138,9 +153,7 @@
     grad_hidden = contract_features(flat_grad, weight_out)
     grad_preact = gelu_back(grad_hidden)[0].astype(bf16)
     half = grad_preact.shape[1] // 2
-    in_term = jnp.concatenate(
-        [contract_cells(scaled, grad_preact[:, :half]), contract_cells(scaled, grad_preact[:, half:])], axis=0
-    )
+    in_term = contract_cells(scaled, grad_preact[:, :half]), contract_cells(scaled, grad_preact[:, half:])
     grad_scaled = contract_features(grad_preact, weight_in)
     gain_term = jnp.sum(grad_scaled * normed, axis=0)
     grad_normed = grad_scaled * norm_gain
@@ -151,29 +164,42 @@
     ) * inverse
     grad_field = grad_filtered.reshape(row_count, col_count, channels)
     conv_term = jnp.sum(grad_field[:, None] * responses, axis=(0, 2))
-    grad_rounded = grad_field.astype(bf16).astype(f32)
-    weighted = (conv_weight[None, :, None, :] * grad_rounded[:, None]).astype(bf16)
-    weighted = weighted.reshape(row_count, K * col_count, channels)
-    parts = jnp.einsum("rmw,rmc->rwc", bands, weighted, preferred_element_type=f32)
-    parts = parts.reshape(row_count, SPAN, padded, channels)
-    spread_out = jnp.zeros((row_count, padded, channels), f32)
-    for at in range(SPAN):
-        by = at - REACH
-        low, high = max(0, -by), row_count - max(0, by)
-        spread_out = spread_out + jnp.pad(
-            parts[low:high, at], ((max(0, by), max(0, -by)), (0, 0), (0, 0))
+
+    def adjoint(grad_rounded):
+        grad_rounded = grad_rounded.astype(f32)
+        weighted = (conv_weight[None, :, None, :] * grad_rounded[:, None]).astype(bf16)
+        weighted = weighted.reshape(row_count, K * col_count, channels)
+        parts = jnp.einsum("rmw,rmc->rwc", bands, weighted, preferred_element_type=f32)
+        parts = parts.reshape(row_count, SPAN, padded, channels)
+        spread_out = jnp.zeros((row_count, padded, channels), f32)
+        for at in range(SPAN):
+            by = at - REACH
+            low, high = max(0, -by), row_count - max(0, by)
+            spread_out = spread_out + jnp.pad(
+                parts[low:high, at], ((max(0, by), max(0, -by)), (0, 0), (0, 0))
+            )
+        return (
+            spread_out[:, :HMAX].astype(bf16),
+            spread_out[:, col_count + HMAX :].astype(bf16),
+            local_grad.astype(f32) + spread_out[:, HMAX : HMAX + col_count],
         )
-    from_east = shifted(spread_out[:, :HMAX].astype(bf16), SPACE, -1).astype(f32)
-    from_west = shifted(spread_out[:, col_count + HMAX :].astype(bf16), SPACE, 1).astype(f32)
-    interior = spread_out[:, HMAX : HMAX + col_count]
-    interior = interior.at[:, :HMAX].add(from_west)
-    interior = interior.at[:, col_count - HMAX :].add(from_east)
-    grad_state = (local_grad.astype(f32) + interior).astype(bf16)[None]
+
+    def send(work):
+        return shifted(work[0], SPACE, -1), shifted(work[1], SPACE, 1)
+
+    def finish(work, sent):
+        interior = work[2]
+        from_east, from_west = sent[0].astype(f32), sent[1].astype(f32)
+        interior = interior.at[:, :HMAX].add(from_west)
+        interior = interior.at[:, col_count - HMAX :].add(from_east)
+        return interior.astype(bf16)[None]
+
     extras = jnp.concatenate(
         [conv_term, gain_term[None], jnp.zeros((EXTRA - K - 1, channels), f32)], axis=0
     )
-    in_total, grad_out, extra_total = reduce_all(in_term, out_term, extras, factor)
-    grad_in = jnp.concatenate([in_total[:channels], in_total[channels:]], axis=1)
+    grad_in, grad_out, extra_total, grad_state = reduce_all(
+        in_term, out_term, extras, factor, (grad_field.astype(bf16), adjoint, send, finish)
+    )
     return (grad_state, extra_total[:K], extra_total[K], grad_in, grad_out)
 
 

time: 124 us -> 116 us (0.935)
  blocking collectives: 13.8 us -> 23.4 us
  starting transfers between devices: 54.2 us -> 47.4 us
  other arithmetic: 9.7 us -> 5.91 us
  local copies, waits for them, and re-layouts: 9.16 us -> 5.58 us
  matrix products: 8.77 us -> 6.8 us
  waiting for transfers between devices: 26.5 us -> 24.9 us
    all_to_all x1 -> x2, blocking collectives: 13.8 us -> 23.4 us  [exchange(): return lax.all_to_all(blocks, axes, 0, 0, tiled=True)]
    all_to_all x4 -> x3, starting transfers between devices: 16.2 us -> 10.2 us  [exchange(): return lax.all_to_all(blocks, axes, 0, 0, tiled=True)]
    all_to_all x4 -> x3, waiting for transfers between devices: 17.7 us -> 11.8 us  [exchange(): return lax.all_to_all(blocks, axes, 0, 0, tiled=True)]
    ppermute x4, waiting for transfers between devices: 7.17 us -> 11.4 us  [shifted(): lax.ppermute(value, axes, [(i, (i + by) % count) for i in range(count)])]
    squeeze x2, local copies, waits for them, and re-layouts: 3.4 us -> 0.28 us  [adjoint(): parts[low:high, at]]
    another operation x5 -> x1, other arithmetic: 2.85 us -> 0.42 us
    dot_general x1, matrix products: 3.73 us -> 1.77 us  [adjoint(): jnp.einsum('rmw,rmc->rwc', bands, weighted, preferred_element_type=f32)]
    ppermute x4, starting transfers between devices: 26.3 us -> 24.6 us  [shifted(): lax.ppermute(value, axes, [(i, (i + by) % count) for i in range(count)])]
  transfers between devices with their start and end apart: 10 -> 9, of which waited for: 5 -> 6; matrix products, arithmetic and copies ran while one was open for 13% -> 7% of each run, Pallas kernels for 0% -> 0%
where the time goes in v2:
time: 116 us; the launch traced here: 115 us
  starting transfers between devices  47.4 us (41%)
  waiting for transfers between devices  24.9 us (21%)
  blocking collectives  23.4 us (20%)
  matrix products  6.8 us (6%)
  other arithmetic  5.91 us (5%)
  local copies, waits for them, and re-layouts  5.58 us (5%)
  between operations  1.26 us (1%)
    ppermute x4, starting transfers between devices, shifted(): lax.ppermute(value, axes, [(i, (i + by) % count) for i in range(count)])  24.6 us
    all_to_all x2, blocking collectives, exchange(): return lax.all_to_all(blocks, axes, 0, 0, tiled=True)  23.4 us
    ppermute x2, starting transfers between devices, swap_cores(): return lax.ppermute(value, 'core', [(0, 1), (1, 0)])  12.6 us
    all_to_all x3, waiting for transfers between devices, exchange(): return lax.all_to_all(blocks, axes, 0, 0, tiled=True)  11.8 us
    ppermute x4, waiting for transfers between devices, shifted(): lax.ppermute(value, axes, [(i, (i + by) % count) for i in range(count)])  11.4 us
    all_to_all x3, starting transfers between devices, exchange(): return lax.all_to_all(blocks, axes, 0, 0, tiled=True)  10.2 us
  transfers between devices with their start and end apart: 9, of which 6 were waited for; matrix products, arithmetic and copies ran while one was open for 7% of the time, Pallas kernels for 0%

profile of v2, /device:TPU:1, one launch (start us, length us, event | category | flops | bytes accessed | tf_op | source)
XLA Modules:
  0.0 115.2 jit_solution(2902432875719777691)
XLA Ops:
  0.7 14.8 %collective-permute-start.1 = (bf16[16,16,384]{2,1,0:T(8,128)(2,1)}, bf16[16,16,384]{2,1,0:T(8,128)(2,1)S(1)}, u32[]{:S(2)}, u32[]{:S(2)}) collective-permute-start(bf16[16,16,384]{2,1,0:T(8,128)(2,1)} %bitcast.155), channel_id=1, source_target_pairs={{0,504},{8,0},{16,8},{24,16},{32,24},{40,32},{48,40},{56,48},{64,5... | collective-permute-start | bytes 589832 | tf_op jit(solution)/shard_map/ppermute | solution.py:24
  15.5 1.9 %collective-permute-start = (bf16[16,16,384]{2,1,0:T(8,128)(2,1)}, bf16[16,16,384]{2,1,0:T(8,128)(2,1)S(1)}, u32[]{:S(2)}, u32[]{:S(2)}) collective-permute-start(bf16[16,16,384]{2,1,0:T(8,128)(2,1)} %bitcast.156), channel_id=1, source_target_pairs={{0,8},{8,16},{16,24},{24,32},{32,40},{40,48},{48,56},{56,64},{64,7... | collective-permute-start | bytes 589832 | tf_op jit(solution)/shard_map/ppermute | solution.py:24
  17.5 0.8 copy.25
  18.5 1.6 %fusion.50 = f32[256,768]{1,0:T(8,128)S(1)} fusion(bf16[256,384]{1,0:T(8,128)(2,1)} %bitcast.133, bf16[768,384]{1,0:T(8,128)(2,1)} %param.23), kind=kOutput, calls=%fused_computation.134 | convolution fusion | flops 150994944 | bytes 1572864 | tf_op jit(solution)/shard_map/dot_general | solution.py:119
  20.1 7.2 %collective-permute-done = bf16[16,16,384]{2,1,0:T(8,128)(2,1)S(1)} collective-permute-done((bf16[16,16,384]{2,1,0:T(8,128)(2,1)}, bf16[16,16,384]{2,1,0:T(8,128)(2,1)S(1)}, u32[]{:S(2)}, u32[]{:S(2)}) %collective-permute-start) | collective-permute-done | bytes 196640 | tf_op jit(solution)/shard_map/ppermute | solution.py:24
  28.6 1.2 %multiply_reduce_fusion = (f32[16,64]{1,0:T(8,128)S(1)}, f32[16,64,384]{2,1,0:T(8,128)S(1)}) fusion(f32[64,384]{1,0:T(8,128)S(1)} %bitcast.151, bf16[16,240,384]{2,1,0:T(8,128)(2,1)S(1)} %bitcast_dynamic-update-slice_fusion, s32[64]{0:T(128)S(1)} %get-tuple-element.131, s32[64]{0:T(128)S(1)} %get-tuple-element.133, f32[16]{0:T(128)S(1)} %get-tuple-element.117, ...), kind=kOutput, calls=%fused_computation.7 | convolution fusion | flops 195918848 | bytes 4634144 | tf_op jit(solution)/shard_map/rmw,rwc->rmc/dot_general | solution.py:136
  33.8 3.8 %collective-permute-start.2 = (bf16[776,384]{1,0:T(8,128)(2,1)S(1)}, bf16[776,384]{1,0:T(8,128)(2,1)S(1)}, u32[]{:S(2)}, u32[]{:S(2)}) collective-permute-start(bf16[776,384]{1,0:T(8,128)(2,1)S(1)} %pad_maximum_fusion.3), channel_id=1, source_target_pairs={{0,1},{1,0},{2,3},{3,2},{4,5},{5,4},{6,7},{7,6},{8,9},{9,8},{10,11... | collective-permute-start | bytes 1787912 | tf_op jit(solution)/shard_map/ppermute | solution.py:28
  37.6 1.6 %collective-permute-done.2 = bf16[776,384]{1,0:T(8,128)(2,1)S(1)} collective-permute-done((bf16[776,384]{1,0:T(8,128)(2,1)S(1)}, bf16[776,384]{1,0:T(8,128)(2,1)S(1)}, u32[]{:S(2)}, u32[]{:S(2)}) %collective-permute-start.2) | collective-permute-done | bytes 596000 | tf_op jit(solution)/shard_map/ppermute | solution.py:28
  39.6 0.9 pad_maximum_fusion.2
  40.5 3.5 %all-to-all-start = ((bf16[8,104,384]{2,1,0:T(8,128)(2,1)}), bf16[8,104,384]{2,1,0:T(8,128)(2,1)S(1)}, u32[]{:S(2)}, u32[]{:S(2)}) async-start(bf16[8,104,384]{2,1,0:T(8,128)(2,1)} %pad_maximum_fusion.2), calls=%async_computation | async-start | bytes 1277952 | tf_op jit(solution)/shard_map/all_to_all | solution.py:55
  44.2 1.8 %fusion.40 = f32[16,240,384]{2,1,0:T(8,128)S(1)} fusion(bf16[16,64,384]{2,1,0:T(8,128)(2,1)S(1)} %fusion, s32[64]{0:T(128)S(1)} %get-tuple-element.131, s32[64]{0:T(128)S(1)} %get-tuple-element.133, f32[16]{0:T(128)S(1)} %get-tuple-element.117, f32[16]{0:T(128)S(1)} %get-tuple-element.116, s32[240]{0:T(256)S(1)} %get-tuple-element.127, ...), kind=kOutput, calls=%fused_computation.127 | convolution fusion | flops 195133440 | bytes 6694432 | tf_op jit(solution)/shard_map/rmw,rmc->rwc/dot_general | solution.py:172
  46.8 8.3 %all-to-all-done = bf16[8,104,384]{2,1,0:T(8,128)(2,1)S(1)} async-done(((bf16[8,104,384]{2,1,0:T(8,128)(2,1)}), bf16[8,104,384]{2,1,0:T(8,128)(2,1)S(1)}, u32[]{:S(2)}, u32[]{:S(2)}) %all-to-all-start) | async-done | bytes 639008 | tf_op jit(solution)/shard_map/all_to_all | solution.py:55
  55.2 12.9 %all_to_all.25 = bf16[4,32,384]{2,1,0:T(8,128)(2,1)S(1)} all-to-all(bf16[4,32,384]{2,1,0:T(8,128)(2,1)S(1)} %pad_maximum_fusion.7), channel_id=1, replica_groups=mesh['x'=4,'z'=8,'yl'=2,'yh'=4,'core'=2] {'yh'}, dimensions={0} | all-to-all | bytes 196608 | tf_op jit(solution)/shard_map/all_to_all | solution.py:55
  68.8 3.4 %all-to-all-start.2 = ((bf16[8,32,384]{2,1,0:T(8,128)(2,1)}), bf16[8,32,384]{2,1,0:T(8,128)(2,1)S(1)}, u32[]{:S(2)}, u32[]{:S(2)}) async-start(bf16[8,32,384]{2,1,0:T(8,128)(2,1)} %broadcast_in_dim.32), calls=%async_computation.2 | async-start | bytes 393216 | tf_op jit(solution)/shard_map/all_to_all | solution.py:55
  72.2 6.0 %collective-permute-start.3 = (bf16[16,16,384]{2,1,0:T(8,128)(2,1)S(1)}, bf16[16,16,384]{2,1,0:T(8,128)(2,1)S(1)}, u32[]{:S(2)}, u32[]{:S(2)}) collective-permute-start(bf16[16,16,384]{2,1,0:T(8,128)(2,1)S(1)} %get-tuple-element.68), channel_id=1, source_target_pairs={{0,504},{8,0},{16,8},{24,16},{32,24},{40,32},{48,40},{56,48},{64,5... | collective-permute-start | bytes 589832 | tf_op jit(solution)/shard_map/ppermute | solution.py:24
  78.2 1.9 %collective-permute-start.4 = (bf16[16,16,384]{2,1,0:T(8,128)(2,1)S(1)}, bf16[16,16,384]{2,1,0:T(8,128)(2,1)S(1)}, u32[]{:S(2)}, u32[]{:S(2)}) collective-permute-start(bf16[16,16,384]{2,1,0:T(8,128)(2,1)S(1)} %get-tuple-element.69), channel_id=1, source_target_pairs={{0,8},{8,16},{16,24},{24,32},{32,40},{40,48},{48,56},{56,64},{64,7... | collective-permute-start | bytes 589832 | tf_op jit(solution)/shard_map/ppermute | solution.py:24
  81.4 3.3 %all-to-all-start.3 = ((bf16[4,24,384]{2,1,0:T(8,128)(2,1)}), bf16[4,24,384]{2,1,0:T(8,128)(2,1)S(1)}, u32[]{:S(2)}, u32[]{:S(2)}) async-start(bf16[4,24,384]{2,1,0:T(8,128)(2,1)} %broadcast_in_dim.33), calls=%async_computation.3 | async-start | bytes 147456 | tf_op jit(solution)/shard_map/all_to_all | solution.py:55
  84.7 4.2 %collective-permute-done.4 = bf16[16,16,384]{2,1,0:T(8,128)(2,1)S(1)} collective-permute-done((bf16[16,16,384]{2,1,0:T(8,128)(2,1)S(1)}, bf16[16,16,384]{2,1,0:T(8,128)(2,1)S(1)}, u32[]{:S(2)}, u32[]{:S(2)}) %collective-permute-start.4) | collective-permute-done | bytes 196640 | tf_op jit(solution)/shard_map/ppermute | solution.py:24
  89.0 2.9 %all-to-all-done.3 = bf16[4,24,384]{2,1,0:T(8,128)(2,1)S(1)} async-done(((bf16[4,24,384]{2,1,0:T(8,128)(2,1)}), bf16[4,24,384]{2,1,0:T(8,128)(2,1)S(1)}, u32[]{:S(2)}, u32[]{:S(2)}) %all-to-all-start.3) | async-done | bytes 73760 | tf_op jit(solution)/shard_map/all_to_all | solution.py:55
  92.0 10.5 %all_to_all.26 = bf16[8,96,384]{2,1,0:T(8,128)(2,1)S(1)} all-to-all(bf16[8,96,384]{2,1,0:T(8,128)(2,1)S(1)} %broadcast_in_dim.35), channel_id=1, replica_groups=mesh['x'=4,'z'=8,'yl'=2,'yh'=4,'core'=2] {'x','yl'}, dimensions={0} | all-to-all | bytes 1179648 | tf_op jit(solution)/shard_map/all_to_all | solution.py:55
  102.5 8.8 %collective-permute-start.5 = (bf16[768,384]{1,0:T(8,128)(2,1)S(1)}, bf16[768,384]{1,0:T(8,128)(2,1)S(1)}, u32[]{:S(2)}, u32[]{:S(2)}) collective-permute-start(bf16[768,384]{1,0:T(8,128)(2,1)S(1)} %bitcast.130), channel_id=1, source_target_pairs={{0,1},{1,0},{2,3},{3,2},{4,5},{5,4},{6,7},{7,6},{8,9},{9,8},{10,11... | collective-permute-start | bytes 1769480 | tf_op jit(solution)/shard_map/ppermute | solution.py:28
  112.5 0.7 fusion.26
  113.5 0.9 pad_maximum_fusion.6
  114.4 0.9 pad_maximum_fusion.5
  (98 shorter events, 10.3 us)
Async XLA Ops:
  0.6 30.0 %copy-start = (bf16[384,768]{1,0:T(8,128)(2,1)S(1)}, bf16[384,768]{1,0:T(8,128)(2,1)}, u32[]{:S(2)}) copy-start(bf16[384,768]{1,0:T(8,128)(2,1)} %param.22) | copy-start | bytes 1769476
  0.6 26.6 %copy-start.2 = (bf16[1,16,16,384]{3,2,1,0:T(8,128)(2,1)S(1)}, bf16[1,16,16,384]{3,2,1,0:T(8,128)(2,1)}, u32[]{:S(2)}) copy-start(bf16[1,16,16,384]{3,2,1,0:T(8,128)(2,1)} %param.16) | copy-start | bytes 589828
  0.7 19.4 %copy-start.5 = (s32[16]{0:T(128)S(1)}, s32[16]{0:T(128)}, u32[]{:S(2)}) copy-start(s32[16]{0:T(128)} %param.18) | copy-start | bytes 196
  0.7 19.4 %collective-permute-start.1 = (bf16[16,16,384]{2,1,0:T(8,128)(2,1)}, bf16[16,16,384]{2,1,0:T(8,128)(2,1)S(1)}, u32[]{:S(2)}, u32[]{:S(2)}) collective-permute-start(bf16[16,16,384]{2,1,0:T(8,128)(2,1)} %bitcast.155), channel_id=1, source_target_pairs={{0,504},{8,0},{16,8},{24,16},{32,24},{40,32},{48,40},{56,48},{64,5... | collective-permute-start | bytes 589832 | tf_op jit(solution)/shard_map/ppermute | solution.py:24
  15.5 11.8 %collective-permute-start = (bf16[16,16,384]{2,1,0:T(8,128)(2,1)}, bf16[16,16,384]{2,1,0:T(8,128)(2,1)S(1)}, u32[]{:S(2)}, u32[]{:S(2)}) collective-permute-start(bf16[16,16,384]{2,1,0:T(8,128)(2,1)} %bitcast.156), channel_id=1, source_target_pairs={{0,8},{8,16},{16,24},{24,32},{32,40},{40,48},{48,56},{56,64},{64,7... | collective-permute-start | bytes 589832 | tf_op jit(solution)/shard_map/ppermute | solution.py:24
  27.9 0.7 copy-start.3
  29.8 0.7 copy-start.4
  31.4 1.1 copy-start.1
  33.8 5.4 %collective-permute-start.2 = (bf16[776,384]{1,0:T(8,128)(2,1)S(1)}, bf16[776,384]{1,0:T(8,128)(2,1)S(1)}, u32[]{:S(2)}, u32[]{:S(2)}) collective-permute-start(bf16[776,384]{1,0:T(8,128)(2,1)S(1)} %pad_maximum_fusion.3), channel_id=1, source_target_pairs={{0,1},{1,0},{2,3},{3,2},{4,5},{5,4},{6,7},{7,6},{8,9},{9,8},{10,11... | collective-permute-start | bytes 1787912 | tf_op jit(solution)/shard_map/ppermute | solution.py:28
  40.5 14.6 %all-to-all-start = ((bf16[8,104,384]{2,1,0:T(8,128)(2,1)}), bf16[8,104,384]{2,1,0:T(8,128)(2,1)S(1)}, u32[]{:S(2)}, u32[]{:S(2)}) async-start(bf16[8,104,384]{2,1,0:T(8,128)(2,1)} %pad_maximum_fusion.2), calls=%async_computation | async-start | bytes 1277952 | tf_op jit(solution)/shard_map/all_to_all | solution.py:55
  68.8 11.9 %all-to-all-start.2 = ((bf16[8,32,384]{2,1,0:T(8,128)(2,1)}), bf16[8,32,384]{2,1,0:T(8,128)(2,1)S(1)}, u32[]{:S(2)}, u32[]{:S(2)}) async-start(bf16[8,32,384]{2,1,0:T(8,128)(2,1)} %broadcast_in_dim.32), calls=%async_computation.2 | async-start | bytes 393216 | tf_op jit(solution)/shard_map/all_to_all | solution.py:55
  72.2 12.5 %collective-permute-start.3 = (bf16[16,16,384]{2,1,0:T(8,128)(2,1)S(1)}, bf16[16,16,384]{2,1,0:T(8,128)(2,1)S(1)}, u32[]{:S(2)}, u32[]{:S(2)}) collective-permute-start(bf16[16,16,384]{2,1,0:T(8,128)(2,1)S(1)} %get-tuple-element.68), channel_id=1, source_target_pairs={{0,504},{8,0},{16,8},{24,16},{32,24},{40,32},{48,40},{56,48},{64,5... | collective-permute-start | bytes 589832 | tf_op jit(solution)/shard_map/ppermute | solution.py:24
  78.2 10.8 %collective-permute-start.4 = (bf16[16,16,384]{2,1,0:T(8,128)(2,1)S(1)}, bf16[16,16,384]{2,1,0:T(8,128)(2,1)S(1)}, u32[]{:S(2)}, u32[]{:S(2)}) collective-permute-start(bf16[16,16,384]{2,1,0:T(8,128)(2,1)S(1)} %get-tuple-element.69), channel_id=1, source_target_pairs={{0,8},{8,16},{16,24},{24,32},{32,40},{40,48},{48,56},{56,64},{64,7... | collective-permute-start | bytes 589832 | tf_op jit(solution)/shard_map/ppermute | solution.py:24
  81.4 10.5 %all-to-all-start.3 = ((bf16[4,24,384]{2,1,0:T(8,128)(2,1)}), bf16[4,24,384]{2,1,0:T(8,128)(2,1)S(1)}, u32[]{:S(2)}, u32[]{:S(2)}) async-start(bf16[4,24,384]{2,1,0:T(8,128)(2,1)} %broadcast_in_dim.33), calls=%async_computation.3 | async-start | bytes 147456 | tf_op jit(solution)/shard_map/all_to_all | solution.py:55
  102.5 10.7 %collective-permute-start.5 = (bf16[768,384]{1,0:T(8,128)(2,1)S(1)}, bf16[768,384]{1,0:T(8,128)(2,1)S(1)}, u32[]{:S(2)}, u32[]{:S(2)}) collective-permute-start(bf16[768,384]{1,0:T(8,128)(2,1)S(1)} %bitcast.130), channel_id=1, source_target_pairs={{0,1},{1,0},{2,3},{3,2},{4,5},{5,4},{6,7},{7,6},{8,9},{9,8},{10,11... | collective-permute-start | bytes 1769480 | tf_op jit(solution)/shard_map/ppermute | solution.py:28

commit v3 on v2

--- a/solution.py
+++ b/solution.py
@@ -3,6 +3,8 @@
 import jax
 import jax.numpy as jnp
 from jax import lax
+from jax.experimental import pallas as pl
+from jax.experimental.pallas import tpu as pltpu
 from jax.sharding import Mesh, PartitionSpec as P
 
 K = 4
@@ -69,19 +71,13 @@
     return jnp.broadcast_to(value[None], (count,) + value.shape)
 
 
-def reduce_all(in_term, out_term, extras, factor, beside):
+def reduce_all(mine, theirs, extras, factor, beside):
     seed, adjoint, send, finish = beside
     core = lax.axis_index("core")
-    channels = extras.shape[1]
-    first = jnp.concatenate([in_term[0], out_term[:channels]], axis=0)
-    second = jnp.concatenate([in_term[1], out_term[channels:]], axis=0)
-    rows = 2 * channels
-    mine = jnp.where(core == 0, first, second)
-    theirs = jnp.where(core == 0, second, first).astype(bf16)
-    extras = rounded(extras)
-    got = swap_cores(jnp.concatenate([theirs, extras.astype(bf16)], axis=0)).astype(f32)
+    rows, channels = mine.shape
+    got = swap_cores(theirs).astype(f32)
     mine = mine + got[:rows]
-    extras = extras + got[rows:]
+    extras = rounded(extras) + got[rows : rows + EXTRA]
     rows = rows // 8
     blocks = with_extras(mine.astype(bf16).reshape(8, rows, channels), extras)
     blocks, seed = lax.optimization_barrier((blocks, seed))
@@ -98,17 +94,20 @@
     blocks = copies(total[:rows].astype(bf16), 4)
     rows = rows * 4
     mine = exchange(blocks, ("yh",)).reshape(rows, channels)
-    blocks, sent = lax.optimization_barrier((copies(mine, 8), sent))
+    at = total.shape[0] - EXTRA
+    blocks, sent, grad_conv, grad_gain = lax.optimization_barrier(
+        (copies(mine, 8), sent, total[at : at + K], total[at + K])
+    )
     rows = rows * 8
     mine = exchange(blocks, ("x", "yl")).reshape(rows, channels)
-    mine, sent, work, total = lax.optimization_barrier((mine, sent, work, total))
+    mine, sent, work = lax.optimization_barrier((mine, sent, work))
     other = swap_cores(mine)
     done = finish(work, sent)
     first = jnp.where(core == 0, mine, other)
     second = jnp.where(core == 0, other, mine)
     grad_in = jnp.concatenate([first[:channels], second[:channels]], axis=1)
     grad_out = jnp.concatenate([first[channels:], second[channels:]], axis=0)
-    return grad_in, grad_out, total[total.shape[0] - EXTRA :], done
+    return done, grad_conv, grad_gain, grad_in, grad_out
 
 
 def contract_cells(left, right):
@@ -117,6 +116,114 @@
 
 def contract_features(left, right):
     return lax.dot_general(left, right, (((1,), (1,)), ((), ())), preferred_element_type=f32)
+
+
+def gelu_pair(value):
+    slope = math.sqrt(2.0 / math.pi)
+    square = value * value
+    bend = jnp.tanh(slope * value * (1.0 + 0.044715 * square))
+    gate = 0.5 * (1.0 + bend)
+    back = gate + 0.5 * value * (1.0 - bend * bend) * (slope * (1.0 + 3.0 * 0.044715 * square))
+    return value * gate, back
+
+
+def block_kernel(
+    core_ref, ext_ref, bands_ref, hid_grad_ref, vec_ref, cot_hbm, win_hbm,
+    mine_ref, theirs_ref, extras_ref, grad_ref,
+    cot_ref, win_ref, resp, filt, hid, back, sems,
+):
+    row_count = bands_ref.shape[0]
+    col_count = bands_ref.shape[1] // K
+    channels = ext_ref.shape[1]
+    padded = col_count + 2 * HMAX
+    load_win = pltpu.make_async_copy(win_hbm, win_ref, sems.at[0])
+    load_cot = pltpu.make_async_copy(cot_hbm, cot_ref, sems.at[1])
+    load_win.start()
+    load_cot.start()
+    for r in range(row_count):
+        y = jnp.dot(bands_ref[r], ext_ref[r * padded : (r + SPAN) * padded], preferred_element_type=f32)
+        resp[r] = y
+        mixed = vec_ref[0:1] * y[:col_count]
+        for k in range(1, K):
+            mixed = mixed + vec_ref[k : k + 1] * y[k * col_count : (k + 1) * col_count]
+        filt[r * col_count : (r + 1) * col_count] = mixed
+    flat = filt[...]
+    center = jnp.mean(flat, axis=-1, keepdims=True)
+    offset = flat - center
+    variance = jnp.mean(offset * offset, axis=-1, keepdims=True)
+    inverse = 1.0 / jnp.sqrt(variance + norm_eps)
+    normed = offset * inverse
+    gain = vec_ref[K : K + 1]
+    scaled = (normed * gain).astype(bf16)
+    load_win.wait()
+    preact = jnp.dot(scaled, win_ref[...], preferred_element_type=f32)
+    hidden, slope = gelu_pair(preact)
+    hid[...] = hidden.astype(bf16)
+    grad_preact = (hid_grad_ref[...] * slope).astype(bf16)
+    back[...] = grad_preact
+    grad_scaled = contract_features(grad_preact, win_ref[...])
+    load_cot.wait()
+    cot = cot_ref[...]
+    own = pl.multiple_of(core_ref[0] * channels, 128)
+    other = pl.multiple_of((1 - core_ref[0]) * channels, 128)
+    mine_ref[:channels] = contract_cells(scaled, back[:, pl.ds(own, channels)])
+    mine_ref[channels:] = contract_cells(hid[:, pl.ds(own, channels)], cot)
+    theirs_ref[:channels] = contract_cells(scaled, back[:, pl.ds(other, channels)]).astype(bf16)
+    theirs_ref[channels : 2 * channels] = contract_cells(hid[:, pl.ds(other, channels)], cot).astype(bf16)
+    gain_term = jnp.sum(grad_scaled * normed, axis=0, keepdims=True)
+    grad_normed = grad_scaled * gain
+    grad = (
+        grad_normed
+        - jnp.mean(grad_normed, axis=-1, keepdims=True)
+        - normed * jnp.mean(grad_normed * normed, axis=-1, keepdims=True)
+    ) * inverse
+    grad_ref[...] = grad.astype(bf16)
+    filt[...] = grad
+    sums = [jnp.zeros((col_count, channels), f32)] * K
+    for r in range(row_count):
+        piece = filt[r * col_count : (r + 1) * col_count]
+        for k in range(K):
+            sums[k] = sums[k] + piece * resp[r, k * col_count : (k + 1) * col_count]
+    extras = jnp.concatenate(
+        [jnp.sum(part, axis=0, keepdims=True) for part in sums]
+        + [gain_term, jnp.zeros((2 * EXTRA - K - 1, channels), f32)],
+        axis=0,
+    )
+    extras_ref[...] = extras[:EXTRA]
+    theirs_ref[2 * channels :] = extras.astype(bf16)
+
+
+def block(extended, bands, hidden_grad, vectors, cotangent, weight_in):
+    row_count = bands.shape[0]
+    col_count = bands.shape[1] // K
+    cells = row_count * col_count
+    channels, wide = weight_in.shape
+    vmem = pl.BlockSpec(memory_space=pltpu.VMEM)
+    core = lax.axis_index("core").astype(jnp.int32)[None]
+    return pl.pallas_call(
+        block_kernel,
+        out_shape=(
+            jax.ShapeDtypeStruct((2 * channels, channels), f32),
+            jax.ShapeDtypeStruct((2 * channels + 2 * EXTRA, channels), bf16),
+            jax.ShapeDtypeStruct((EXTRA, channels), f32),
+            jax.ShapeDtypeStruct((cells, channels), bf16),
+        ),
+        in_specs=[pl.BlockSpec(memory_space=pltpu.SMEM)] + [vmem] * 4 + [pl.BlockSpec(memory_space=pl.ANY)] * 2,
+        out_specs=(vmem,) * 4,
+        scratch_shapes=[
+            pltpu.VMEM((cells, channels), bf16),
+            pltpu.VMEM((channels, wide), bf16),
+            pltpu.VMEM((row_count, K * col_count, channels), f32),
+            pltpu.VMEM((cells, channels), f32),
+            pltpu.VMEM((cells, wide), bf16),
+            pltpu.VMEM((cells, wide), bf16),
+            pltpu.SemaphoreType.DMA((2,)),
+        ],
+        compiler_params=pltpu.CompilerParams(vmem_limit_bytes=32 * 1024 * 1024),
+        cost_estimate=pl.CostEstimate(
+            flops=10 * cells * channels * wide, bytes_accessed=4 * channels * wide, transcendentals=cells * wide
+        ),
+    )(core, extended, bands, hidden_grad, vectors, cotangent, weight_in)
 
 
 def on_device(state, cotangent, halo_cols, row_offset, conv_weight, norm_gain, weight_in, weight_out):
@@ -127,46 +234,18 @@
     west = shifted(local_state[:, col_count - HMAX :], SPACE, 1)
     east = shifted(local_state[:, :HMAX], SPACE, -1)
     bands = band_blocks(halo_cols, row_offset, row_count, col_count)
-    extended = jnp.pad(
-        jnp.concatenate([west, local_state, east], axis=1), ((REACH, REACH), (0, 0), (0, 0))
-    )
-    windows = jnp.stack(
-        [extended[r : r + SPAN].reshape(SPAN * padded, channels) for r in range(row_count)]
-    )
-    responses = jnp.einsum("rmw,rwc->rmc", bands, windows, preferred_element_type=f32)
-    responses = responses.reshape(row_count, K, col_count, channels)
-    filtered = jnp.sum(conv_weight[None, :, None, :] * responses, axis=1)
     cell_count = row_count * col_count
-    flat_mixed = filtered.reshape(cell_count, channels)
-    center = jnp.mean(flat_mixed, axis=-1, keepdims=True)
-    offset_vals = flat_mixed - center
-    variance = jnp.mean(offset_vals * offset_vals, axis=-1, keepdims=True)
-    inverse = 1.0 / jnp.sqrt(variance + norm_eps)
-    normed = offset_vals * inverse
-    scaled = (normed * norm_gain).astype(bf16)
-    preact = jnp.dot(scaled, weight_in, preferred_element_type=f32)
-    hidden_vals, gelu_back = jax.vjp(jax.nn.gelu, preact)
-    hidden = hidden_vals.astype(bf16)
+    factor = 1.0 / math.sqrt(lax.axis_size(ENS) * cell_count * lax.axis_size(SPACE))
     flat_grad = local_grad.reshape(cell_count, channels)
-    factor = 1.0 / math.sqrt(lax.axis_size(ENS) * cell_count * lax.axis_size(SPACE))
-    out_term = contract_cells(hidden, flat_grad)
-    grad_hidden = contract_features(flat_grad, weight_out)
-    grad_preact = gelu_back(grad_hidden)[0].astype(bf16)
-    half = grad_preact.shape[1] // 2
-    in_term = contract_cells(scaled, grad_preact[:, :half]), contract_cells(scaled, grad_preact[:, half:])
-    grad_scaled = contract_features(grad_preact, weight_in)
-    gain_term = jnp.sum(grad_scaled * normed, axis=0)
-    grad_normed = grad_scaled * norm_gain
-    grad_filtered = (
-        grad_normed
-        - jnp.mean(grad_normed, axis=-1, keepdims=True)
-        - normed * jnp.mean(grad_normed * normed, axis=-1, keepdims=True)
-    ) * inverse
-    grad_field = grad_filtered.reshape(row_count, col_count, channels)
-    conv_term = jnp.sum(grad_field[:, None] * responses, axis=(0, 2))
+    extended = jnp.concatenate([west, local_state, east], axis=1)
+    extended = jnp.pad(extended, ((REACH, REACH), (0, 0), (0, 0))).reshape(-1, channels)
+    vectors = jnp.concatenate([conv_weight, norm_gain[None], jnp.zeros((8 - K - 1, channels), f32)], axis=0)
+    mine, theirs, extras, grad_field = block(
+        extended, bands, contract_features(flat_grad, weight_out), vectors, flat_grad, weight_in
+    )
 
     def adjoint(grad_rounded):
-        grad_rounded = grad_rounded.astype(f32)
+        grad_rounded = grad_rounded.astype(f32).reshape(row_count, col_count, channels)
         weighted = (conv_weight[None, :, None, :] * grad_rounded[:, None]).astype(bf16)
         weighted = weighted.reshape(row_count, K * col_count, channels)
         parts = jnp.einsum("rmw,rmc->rwc", bands, weighted, preferred_element_type=f32)
@@ -194,13 +273,7 @@
         interior = interior.at[:, col_count - HMAX :].add(from_east)
         return interior.astype(bf16)[None]
 
-    extras = jnp.concatenate(
-        [conv_term, gain_term[None], jnp.zeros((EXTRA - K - 1, channels), f32)], axis=0
-    )
-    grad_in, grad_out, extra_total, grad_state = reduce_all(
-        in_term, out_term, extras, factor, (grad_field.astype(bf16), adjoint, send, finish)
-    )
-    return (grad_state, extra_total[:K], extra_total[K], grad_in, grad_out)
+    return reduce_all(mine, theirs, extras, factor, (grad_field, adjoint, send, finish))
 
 
 def solution(mesh):

time: 116 us -> 113 us (0.974)
  matrix products: 6.8 us -> 3.08 us
  Pallas kernels: 0 us -> 3.06 us
  waiting for transfers between devices: 24.9 us -> 23.4 us
    ppermute x4, waiting for transfers between devices: 11.4 us -> 8.24 us  [shifted(): lax.ppermute(value, axes, [(i, (i + by) % count) for i in range(count)])]
    pallas_call x0 -> x1, Pallas kernels: none -> 3.06 us  [block(): pl.pallas_call(block_kernel, out_shape=(jax.ShapeDtypeStruct((2 * channel...]
    dot_general x5 -> x0, matrix products: 2.95 us -> none  [the longest x1 1.21 us: on_device(): jnp.einsum('rmw,rwc->rmc', bands, windows, preferred_element_type=f32)]
  transfers between devices with their start and end apart: 9 -> 9, of which waited for: 6 -> 7; matrix products, arithmetic and copies ran while one was open for 7% -> 9% of each run, Pallas kernels for 0% -> 0%
where the time goes in v3:
time: 113 us; the launch traced here: 112 us
  starting transfers between devices  47.4 us (42%)
  waiting for transfers between devices  23.4 us (21%)
  blocking collectives  23.3 us (21%)
  other arithmetic  5.97 us (5%)
  local copies, waits for them, and re-layouts  4.78 us (4%)
  matrix products  3.08 us (3%)
  Pallas kernels  3.06 us (3%)
    ppermute x4, starting transfers between devices, shifted(): lax.ppermute(value, axes, [(i, (i + by) % count) for i in range(count)])  24.6 us
    all_to_all x2, blocking collectives, exchange(): return lax.all_to_all(blocks, axes, 0, 0, tiled=True)  23.3 us
    all_to_all x3, waiting for transfers between devices, exchange(): return lax.all_to_all(blocks, axes, 0, 0, tiled=True)  12.7 us
    ppermute x2, starting transfers between devices, swap_cores(): return lax.ppermute(value, 'core', [(0, 1), (1, 0)])  12.6 us
    all_to_all x3, starting transfers between devices, exchange(): return lax.all_to_all(blocks, axes, 0, 0, tiled=True)  10.2 us
    ppermute x4, waiting for transfers between devices, shifted(): lax.ppermute(value, axes, [(i, (i + by) % count) for i in range(count)])  8.24 us
    pallas_call x1, Pallas kernels, block(): pl.pallas_call(block_kernel, out_shape=(jax.ShapeDtypeStruct((2 * channel...  3.06 us
    ppermute x2, waiting for transfers between devices, swap_cores(): return lax.ppermute(value, 'core', [(0, 1), (1, 0)])  2.49 us
  transfers between devices with their start and end apart: 9, of which 7 were waited for; matrix products, arithmetic and copies ran while one was open for 9% of the time, Pallas kernels for 0%

profile of v3, /device:TPU:1, one launch (start us, length us, event | category | flops | bytes accessed | tf_op | source)
XLA Modules:
  0.0 112.1 jit_solution(16107482130983239767)
XLA Ops:
  0.7 14.8 %collective-permute-start.1 = (bf16[16,16,384]{2,1,0:T(8,128)(2,1)}, bf16[16,16,384]{2,1,0:T(8,128)(2,1)S(1)}, u32[]{:S(2)}, u32[]{:S(2)}) collective-permute-start(bf16[16,16,384]{2,1,0:T(8,128)(2,1)} %bitcast.64), channel_id=1, source_target_pairs={{0,504},{8,0},{16,8},{24,16},{32,24},{40,32},{48,40},{56,48},{64,5... | collective-permute-start | bytes 589832 | tf_op jit(solution)/shard_map/ppermute | solution.py:26
  15.5 1.9 %collective-permute-start = (bf16[16,16,384]{2,1,0:T(8,128)(2,1)}, bf16[16,16,384]{2,1,0:T(8,128)(2,1)S(1)}, u32[]{:S(2)}, u32[]{:S(2)}) collective-permute-start(bf16[16,16,384]{2,1,0:T(8,128)(2,1)} %bitcast.65), channel_id=1, source_target_pairs={{0,8},{8,16},{16,24},{24,32},{32,40},{40,48},{48,56},{56,64},{64,7... | collective-permute-start | bytes 589832 | tf_op jit(solution)/shard_map/ppermute | solution.py:26
  18.9 0.8 copy.19
  19.9 1.3 %fusion.30.hid_grad_ref = f32[256,768]{1,0:T(8,128)S(1)} fusion(bf16[256,384]{1,0:T(8,128)(2,1)} %bitcast.52, bf16[768,384]{1,0:T(8,128)(2,1)S(1)} %copy-done), kind=kOutput, calls=%fused_computation.73 | convolution fusion | flops 150994944 | bytes 1572864 | tf_op jit(solution)/shard_map/dot_general | solution.py:118
  21.9 5.4 %collective-permute-done = bf16[16,16,384]{2,1,0:T(8,128)(2,1)S(1)} collective-permute-done((bf16[16,16,384]{2,1,0:T(8,128)(2,1)}, bf16[16,16,384]{2,1,0:T(8,128)(2,1)S(1)}, u32[]{:S(2)}, u32[]{:S(2)}) %collective-permute-start) | collective-permute-done | bytes 196640 | tf_op jit(solution)/shard_map/ppermute | solution.py:26
  27.4 3.1 %shard_map.129 = (f32[768,384]{1,0:T(8,128)S(1)}, bf16[784,384]{1,0:T(8,128)(2,1)S(1)}, f32[8,384]{1,0:T(8,128)S(1)}, bf16[256,384]{1,0:T(8,128)(2,1)S(1)}) custom-call(s32[1]{0:T(128)} %bitcast.core_ref, bf16[960,384]{1,0:T(8,128)(2,1)S(1)} %bitcast.51, bf16[16,64,240]{2,1,0:T(8,128)(2,1)S(1)} %fusion.11.bands_ref, f32[256,768]{1,0:T(8,128)S(1)} %fusion.30.hid_grad_ref, ...), custom_call_target="tpu_custom_call" | custom-call | flops 754974720 | bytes 1179648 | tf_op jit(solution)/shard_map/pallas_call | solution.py:203
  30.5 3.8 %collective-permute-start.2 = (bf16[784,384]{1,0:T(8,128)(2,1)S(1)}, bf16[784,384]{1,0:T(8,128)(2,1)S(1)}, u32[]{:S(2)}, u32[]{:S(2)}) collective-permute-start(bf16[784,384]{1,0:T(8,128)(2,1)S(1)} %get-tuple-element.68), channel_id=1, source_target_pairs={{0,1},{1,0},{2,3},{3,2},{4,5},{5,4},{6,7},{7,6},{8,9},{9,8},{10,11... | collective-permute-start | bytes 1806344 | tf_op jit(solution)/shard_map/ppermute | solution.py:30
  34.2 1.6 %collective-permute-done.2 = bf16[784,384]{1,0:T(8,128)(2,1)S(1)} collective-permute-done((bf16[784,384]{1,0:T(8,128)(2,1)S(1)}, bf16[784,384]{1,0:T(8,128)(2,1)S(1)}, u32[]{:S(2)}, u32[]{:S(2)}) %collective-permute-start.2) | collective-permute-done | bytes 602144 | tf_op jit(solution)/shard_map/ppermute | solution.py:30
  36.1 0.9 pad_maximum_fusion
  37.0 3.5 %all-to-all-start = ((bf16[8,104,384]{2,1,0:T(8,128)(2,1)}), bf16[8,104,384]{2,1,0:T(8,128)(2,1)S(1)}, u32[]{:S(2)}, u32[]{:S(2)}) async-start(bf16[8,104,384]{2,1,0:T(8,128)(2,1)} %pad_maximum_fusion), calls=%async_computation | async-start | bytes 1277952 | tf_op jit(solution)/shard_map/all_to_all | solution.py:57
  40.8 1.8 %fusion.23 = f32[16,240,384]{2,1,0:T(8,128)S(1)} fusion(bf16[16,64,384]{2,1,0:T(8,128)(2,1)S(1)} %fusion, s32[64]{0:T(128)S(1)} %get-tuple-element.113, s32[64]{0:T(128)S(1)} %get-tuple-element.115, f32[16]{0:T(128)S(1)} %get-tuple-element.104, f32[16]{0:T(128)S(1)} %get-tuple-element.103, s32[240]{0:T(256)S(1)} %get-tuple-element.109, ...), kind=kOutput, calls=%fused_computation.68 | convolution fusion | flops 195133440 | bytes 6694432 | tf_op jit(solution)/shard_map/rmw,rmc->rwc/dot_general | solution.py:251
  43.4 8.2 %all-to-all-done = bf16[8,104,384]{2,1,0:T(8,128)(2,1)S(1)} async-done(((bf16[8,104,384]{2,1,0:T(8,128)(2,1)}), bf16[8,104,384]{2,1,0:T(8,128)(2,1)S(1)}, u32[]{:S(2)}, u32[]{:S(2)}) %all-to-all-start) | async-done | bytes 639008 | tf_op jit(solution)/shard_map/all_to_all | solution.py:57
  51.8 12.9 %all_to_all.25 = bf16[4,32,384]{2,1,0:T(8,128)(2,1)S(1)} all-to-all(bf16[4,32,384]{2,1,0:T(8,128)(2,1)S(1)} %pad_maximum_fusion.3), channel_id=1, replica_groups=mesh['x'=4,'z'=8,'yl'=2,'yh'=4,'core'=2] {'yh'}, dimensions={0} | all-to-all | bytes 196608 | tf_op jit(solution)/shard_map/all_to_all | solution.py:57
  65.4 3.4 %all-to-all-start.2 = ((bf16[8,32,384]{2,1,0:T(8,128)(2,1)}), bf16[8,32,384]{2,1,0:T(8,128)(2,1)S(1)}, u32[]{:S(2)}, u32[]{:S(2)}) async-start(bf16[8,32,384]{2,1,0:T(8,128)(2,1)} %broadcast_in_dim.61), calls=%async_computation.2 | async-start | bytes 393216 | tf_op jit(solution)/shard_map/all_to_all | solution.py:57
  68.8 6.0 %collective-permute-start.3 = (bf16[16,16,384]{2,1,0:T(8,128)(2,1)S(1)}, bf16[16,16,384]{2,1,0:T(8,128)(2,1)S(1)}, u32[]{:S(2)}, u32[]{:S(2)}) collective-permute-start(bf16[16,16,384]{2,1,0:T(8,128)(2,1)S(1)} %get-tuple-element.77), channel_id=1, source_target_pairs={{0,504},{8,0},{16,8},{24,16},{32,24},{40,32},{48,40},{56,48},{64,5... | collective-permute-start | bytes 589832 | tf_op jit(solution)/shard_map/ppermute | solution.py:26
  74.7 1.9 %collective-permute-start.4 = (bf16[16,16,384]{2,1,0:T(8,128)(2,1)S(1)}, bf16[16,16,384]{2,1,0:T(8,128)(2,1)S(1)}, u32[]{:S(2)}, u32[]{:S(2)}) collective-permute-start(bf16[16,16,384]{2,1,0:T(8,128)(2,1)S(1)} %get-tuple-element.78), channel_id=1, source_target_pairs={{0,8},{8,16},{16,24},{24,32},{32,40},{40,48},{48,56},{56,64},{64,7... | collective-permute-start | bytes 589832 | tf_op jit(solution)/shard_map/ppermute | solution.py:26
  78.6 3.3 %all-to-all-start.3 = ((bf16[4,24,384]{2,1,0:T(8,128)(2,1)}), bf16[4,24,384]{2,1,0:T(8,128)(2,1)S(1)}, u32[]{:S(2)}, u32[]{:S(2)}) async-start(bf16[4,24,384]{2,1,0:T(8,128)(2,1)} %broadcast_in_dim.62), calls=%async_computation.3 | async-start | bytes 147456 | tf_op jit(solution)/shard_map/all_to_all | solution.py:57
  82.5 2.9 %collective-permute-done.4 = bf16[16,16,384]{2,1,0:T(8,128)(2,1)S(1)} collective-permute-done((bf16[16,16,384]{2,1,0:T(8,128)(2,1)S(1)}, bf16[16,16,384]{2,1,0:T(8,128)(2,1)S(1)}, u32[]{:S(2)}, u32[]{:S(2)}) %collective-permute-start.4) | collective-permute-done | bytes 196640 | tf_op jit(solution)/shard_map/ppermute | solution.py:26
  85.4 3.8 %all-to-all-done.3 = bf16[4,24,384]{2,1,0:T(8,128)(2,1)S(1)} async-done(((bf16[4,24,384]{2,1,0:T(8,128)(2,1)}), bf16[4,24,384]{2,1,0:T(8,128)(2,1)S(1)}, u32[]{:S(2)}, u32[]{:S(2)}) %all-to-all-start.3) | async-done | bytes 73760 | tf_op jit(solution)/shard_map/all_to_all | solution.py:57
  89.2 10.5 %all_to_all.26 = bf16[8,96,384]{2,1,0:T(8,128)(2,1)S(1)} all-to-all(bf16[8,96,384]{2,1,0:T(8,128)(2,1)S(1)} %broadcast_in_dim.64), channel_id=1, replica_groups=mesh['x'=4,'z'=8,'yl'=2,'yh'=4,'core'=2] {'x','yl'}, dimensions={0} | all-to-all | bytes 1179648 | tf_op jit(solution)/shard_map/all_to_all | solution.py:57
  99.7 8.8 %collective-permute-start.5 = (bf16[768,384]{1,0:T(8,128)(2,1)S(1)}, bf16[768,384]{1,0:T(8,128)(2,1)S(1)}, u32[]{:S(2)}, u32[]{:S(2)}) collective-permute-start(bf16[768,384]{1,0:T(8,128)(2,1)S(1)} %bitcast.58), channel_id=1, source_target_pairs={{0,1},{1,0},{2,3},{3,2},{4,5},{5,4},{6,7},{7,6},{8,9},{9,8},{10,11... | collective-permute-start | bytes 1769480 | tf_op jit(solution)/shard_map/ppermute | solution.py:30
  109.2 0.9 collective-permute-done.5
  110.3 0.9 pad_maximum_fusion.2
  111.2 0.9 pad_maximum_fusion.1
  (60 shorter events, 8.0 us)
Async XLA Ops:
  0.6 19.3 %copy-start = (bf16[768,384]{1,0:T(8,128)(2,1)S(1)}, bf16[768,384]{1,0:T(8,128)(2,1)}, u32[]{:S(2)}) copy-start(bf16[768,384]{1,0:T(8,128)(2,1)} %param.23) | copy-start | bytes 1769476
  0.6 26.7 %copy-start.3 = (bf16[1,16,16,384]{3,2,1,0:T(8,128)(2,1)S(1)}, bf16[1,16,16,384]{3,2,1,0:T(8,128)(2,1)}, u32[]{:S(2)}) copy-start(bf16[1,16,16,384]{3,2,1,0:T(8,128)(2,1)} %param.16) | copy-start | bytes 589828
  0.7 20.6 %copy-start.5 = (s32[16]{0:T(128)S(1)}, s32[16]{0:T(128)}, u32[]{:S(2)}) copy-start(s32[16]{0:T(128)} %param.18) | copy-start | bytes 196
  0.7 21.2 %copy-start.4 = (f32[4,384]{1,0:T(4,128)S(1)}, f32[4,384]{1,0:T(4,128)}, u32[]{:S(2)}) copy-start(f32[4,384]{1,0:T(4,128)} %param.20) | copy-start | bytes 18436
  0.7 21.2 %collective-permute-start.1 = (bf16[16,16,384]{2,1,0:T(8,128)(2,1)}, bf16[16,16,384]{2,1,0:T(8,128)(2,1)S(1)}, u32[]{:S(2)}, u32[]{:S(2)}) collective-permute-start(bf16[16,16,384]{2,1,0:T(8,128)(2,1)} %bitcast.64), channel_id=1, source_target_pairs={{0,504},{8,0},{16,8},{24,16},{32,24},{40,32},{48,40},{56,48},{64,5... | collective-permute-start | bytes 589832 | tf_op jit(solution)/shard_map/ppermute | solution.py:26
  15.5 11.8 %collective-permute-start = (bf16[16,16,384]{2,1,0:T(8,128)(2,1)}, bf16[16,16,384]{2,1,0:T(8,128)(2,1)S(1)}, u32[]{:S(2)}, u32[]{:S(2)}) collective-permute-start(bf16[16,16,384]{2,1,0:T(8,128)(2,1)} %bitcast.65), channel_id=1, source_target_pairs={{0,8},{8,16},{16,24},{24,32},{32,40},{40,48},{48,56},{56,64},{64,7... | collective-permute-start | bytes 589832 | tf_op jit(solution)/shard_map/ppermute | solution.py:26
  21.2 6.2 %copy-start.1 = (bf16[1,16,16,384]{3,2,1,0:T(8,128)(2,1)S(1)}, bf16[1,16,16,384]{3,2,1,0:T(8,128)(2,1)}, u32[]{:S(2)}) copy-start(bf16[1,16,16,384]{3,2,1,0:T(8,128)(2,1)} %param.17) | copy-start | bytes 589828
  21.2 6.2 %copy-start.2 = (bf16[384,768]{1,0:T(8,128)(2,1)S(1)}, bf16[384,768]{1,0:T(8,128)(2,1)}, u32[]{:S(2)}) copy-start(bf16[384,768]{1,0:T(8,128)(2,1)} %win_hbm.1) | copy-start | bytes 1769476
  30.5 5.4 %collective-permute-start.2 = (bf16[784,384]{1,0:T(8,128)(2,1)S(1)}, bf16[784,384]{1,0:T(8,128)(2,1)S(1)}, u32[]{:S(2)}, u32[]{:S(2)}) collective-permute-start(bf16[784,384]{1,0:T(8,128)(2,1)S(1)} %get-tuple-element.68), channel_id=1, source_target_pairs={{0,1},{1,0},{2,3},{3,2},{4,5},{5,4},{6,7},{7,6},{8,9},{9,8},{10,11... | collective-permute-start | bytes 1806344 | tf_op jit(solution)/shard_map/ppermute | solution.py:30
  37.0 14.6 %all-to-all-start = ((bf16[8,104,384]{2,1,0:T(8,128)(2,1)}), bf16[8,104,384]{2,1,0:T(8,128)(2,1)S(1)}, u32[]{:S(2)}, u32[]{:S(2)}) async-start(bf16[8,104,384]{2,1,0:T(8,128)(2,1)} %pad_maximum_fusion), calls=%async_computation | async-start | bytes 1277952 | tf_op jit(solution)/shard_map/all_to_all | solution.py:57
  65.4 11.9 %all-to-all-start.2 = ((bf16[8,32,384]{2,1,0:T(8,128)(2,1)}), bf16[8,32,384]{2,1,0:T(8,128)(2,1)S(1)}, u32[]{:S(2)}, u32[]{:S(2)}) async-start(bf16[8,32,384]{2,1,0:T(8,128)(2,1)} %broadcast_in_dim.61), calls=%async_computation.2 | async-start | bytes 393216 | tf_op jit(solution)/shard_map/all_to_all | solution.py:57
  68.8 13.7 %collective-permute-start.3 = (bf16[16,16,384]{2,1,0:T(8,128)(2,1)S(1)}, bf16[16,16,384]{2,1,0:T(8,128)(2,1)S(1)}, u32[]{:S(2)}, u32[]{:S(2)}) collective-permute-start(bf16[16,16,384]{2,1,0:T(8,128)(2,1)S(1)} %get-tuple-element.77), channel_id=1, source_target_pairs={{0,504},{8,0},{16,8},{24,16},{32,24},{40,32},{48,40},{56,48},{64,5... | collective-permute-start | bytes 589832 | tf_op jit(solution)/shard_map/ppermute | solution.py:26
  74.7 10.6 %collective-permute-start.4 = (bf16[16,16,384]{2,1,0:T(8,128)(2,1)S(1)}, bf16[16,16,384]{2,1,0:T(8,128)(2,1)S(1)}, u32[]{:S(2)}, u32[]{:S(2)}) collective-permute-start(bf16[16,16,384]{2,1,0:T(8,128)(2,1)S(1)} %get-tuple-element.78), channel_id=1, source_target_pairs={{0,8},{8,16},{16,24},{24,32},{32,40},{40,48},{48,56},{56,64},{64,7... | collective-permute-start | bytes 589832 | tf_op jit(solution)/shard_map/ppermute | solution.py:26
  78.6 10.6 %all-to-all-start.3 = ((bf16[4,24,384]{2,1,0:T(8,128)(2,1)}), bf16[4,24,384]{2,1,0:T(8,128)(2,1)S(1)}, u32[]{:S(2)}, u32[]{:S(2)}) async-start(bf16[4,24,384]{2,1,0:T(8,128)(2,1)} %broadcast_in_dim.62), calls=%async_computation.3 | async-start | bytes 147456 | tf_op jit(solution)/shard_map/all_to_all | solution.py:57
  99.7 10.4 %collective-permute-start.5 = (bf16[768,384]{1,0:T(8,128)(2,1)S(1)}, bf16[768,384]{1,0:T(8,128)(2,1)S(1)}, u32[]{:S(2)}, u32[]{:S(2)}) collective-permute-start(bf16[768,384]{1,0:T(8,128)(2,1)S(1)} %bitcast.58), channel_id=1, source_target_pairs={{0,1},{1,0},{2,3},{3,2},{4,5},{5,4},{6,7},{7,6},{8,9},{9,8},{10,11... | collective-permute-start | bytes 1769480 | tf_op jit(solution)/shard_map/ppermute | solution.py:30

commit v4 on v3

--- a/solution.py
+++ b/solution.py
@@ -91,22 +91,24 @@
     blocks, edges = lax.optimization_barrier((blocks, work[:2]))
     sent = send(edges)
     total = jnp.sum(exchange(blocks, ("z",)).astype(f32), axis=0) * factor
-    blocks = copies(total[:rows].astype(bf16), 4)
+    blocks, total = lax.optimization_barrier((copies(total[:rows].astype(bf16), 4), total))
+    small = total[rows : rows + K], total[rows + K]
     rows = rows * 4
     mine = exchange(blocks, ("yh",)).reshape(rows, channels)
-    at = total.shape[0] - EXTRA
-    blocks, sent, grad_conv, grad_gain = lax.optimization_barrier(
-        (copies(mine, 8), sent, total[at : at + K], total[at + K])
-    )
+    blocks, sent, small = lax.optimization_barrier((copies(mine, 8), sent, small))
     rows = rows * 8
     mine = exchange(blocks, ("x", "yl")).reshape(rows, channels)
     mine, sent, work = lax.optimization_barrier((mine, sent, work))
     other = swap_cores(mine)
     done = finish(work, sent)
-    first = jnp.where(core == 0, mine, other)
-    second = jnp.where(core == 0, other, mine)
-    grad_in = jnp.concatenate([first[:channels], second[:channels]], axis=1)
-    grad_out = jnp.concatenate([first[channels:], second[channels:]], axis=0)
+    first = jnp.where(core == 0, mine[:channels], other[:channels])
+    second = jnp.where(core == 0, other[:channels], mine[:channels])
+    grad_in = jnp.concatenate([first, second], axis=1)
+    halves = jnp.zeros((2, channels, channels), bf16)
+    halves = lax.dynamic_update_index_in_dim(halves, mine[channels:], core, 0)
+    halves = lax.dynamic_update_index_in_dim(halves, other[channels:], 1 - core, 0)
+    grad_out = halves.reshape(2 * channels, channels)
+    grad_conv, grad_gain = small
     return done, grad_conv, grad_gain, grad_in, grad_out
 
 

time: 113 us -> 112 us (level)
  no operation moved by 1% of the time
where the time goes in v4:
time: 112 us; the launch traced here: 111 us
  starting transfers between devices  47.4 us (42%)
  blocking collectives  23.4 us (21%)
  waiting for transfers between devices  22.6 us (20%)
  local copies, waits for them, and re-layouts  5.63 us (5%)
  other arithmetic  5.05 us (5%)
  matrix products  3.08 us (3%)
  Pallas kernels  3.06 us (3%)
    ppermute x4, starting transfers between devices, shifted(): lax.ppermute(value, axes, [(i, (i + by) % count) for i in range(count)])  24.6 us
    all_to_all x2, blocking collectives, exchange(): return lax.all_to_all(blocks, axes, 0, 0, tiled=True)  23.4 us
    ppermute x2, starting transfers between devices, swap_cores(): return lax.ppermute(value, 'core', [(0, 1), (1, 0)])  12.6 us
    all_to_all x3, waiting for transfers between devices, exchange(): return lax.all_to_all(blocks, axes, 0, 0, tiled=True)  11.8 us
    all_to_all x3, starting transfers between devices, exchange(): return lax.all_to_all(blocks, axes, 0, 0, tiled=True)  10.2 us
    ppermute x4, waiting for transfers between devices, shifted(): lax.ppermute(value, axes, [(i, (i + by) % count) for i in range(count)])  8.43 us
    pallas_call x1, Pallas kernels, block(): pl.pallas_call(block_kernel, out_shape=(jax.ShapeDtypeStruct((2 * channel...  3.06 us
    ppermute x2, waiting for transfers between devices, swap_cores(): return lax.ppermute(value, 'core', [(0, 1), (1, 0)])  2.37 us
  transfers between devices with their start and end apart: 9, of which 7 were waited for; matrix products, arithmetic and copies ran while one was open for 9% of the time, Pallas kernels for 0%

profile of v4, /device:TPU:1, one launch (start us, length us, event | category | flops | bytes accessed | tf_op | source)
XLA Modules:
  0.0 111.3 jit_solution(5064703281337142783)
XLA Ops:
  0.7 14.8 %collective-permute-start.1 = (bf16[16,16,384]{2,1,0:T(8,128)(2,1)}, bf16[16,16,384]{2,1,0:T(8,128)(2,1)S(1)}, u32[]{:S(2)}, u32[]{:S(2)}) collective-permute-start(bf16[16,16,384]{2,1,0:T(8,128)(2,1)} %bitcast.73), channel_id=1, source_target_pairs={{0,504},{8,0},{16,8},{24,16},{32,24},{40,32},{48,40},{56,48},{64,5... | collective-permute-start | bytes 589832 | tf_op jit(solution)/shard_map/ppermute | solution.py:26
  15.5 1.9 %collective-permute-start = (bf16[16,16,384]{2,1,0:T(8,128)(2,1)}, bf16[16,16,384]{2,1,0:T(8,128)(2,1)S(1)}, u32[]{:S(2)}, u32[]{:S(2)}) collective-permute-start(bf16[16,16,384]{2,1,0:T(8,128)(2,1)} %bitcast.74), channel_id=1, source_target_pairs={{0,8},{8,16},{16,24},{24,32},{32,40},{40,48},{48,56},{56,64},{64,7... | collective-permute-start | bytes 589832 | tf_op jit(solution)/shard_map/ppermute | solution.py:26
  18.2 0.8 copy.19
  19.8 1.3 %fusion.29.hid_grad_ref = f32[256,768]{1,0:T(8,128)S(1)} fusion(bf16[256,384]{1,0:T(8,128)(2,1)} %bitcast.59, bf16[768,384]{1,0:T(8,128)(2,1)S(1)} %copy-done), kind=kOutput, calls=%fused_computation.73 | convolution fusion | flops 150994944 | bytes 1572864 | tf_op jit(solution)/shard_map/dot_general | solution.py:120
  21.9 5.4 %collective-permute-done = bf16[16,16,384]{2,1,0:T(8,128)(2,1)S(1)} collective-permute-done((bf16[16,16,384]{2,1,0:T(8,128)(2,1)}, bf16[16,16,384]{2,1,0:T(8,128)(2,1)S(1)}, u32[]{:S(2)}, u32[]{:S(2)}) %collective-permute-start) | collective-permute-done | bytes 196640 | tf_op jit(solution)/shard_map/ppermute | solution.py:26
  27.4 3.1 %shard_map.129 = (f32[768,384]{1,0:T(8,128)S(1)}, bf16[784,384]{1,0:T(8,128)(2,1)S(1)}, f32[8,384]{1,0:T(8,128)S(1)}, bf16[256,384]{1,0:T(8,128)(2,1)S(1)}) custom-call(s32[1]{0:T(128)} %bitcast.core_ref, bf16[960,384]{1,0:T(8,128)(2,1)S(1)} %bitcast.58, bf16[16,64,240]{2,1,0:T(8,128)(2,1)S(1)} %fusion.11.bands_ref, f32[256,768]{1,0:T(8,128)S(1)} %fusion.29.hid_grad_ref, ...), custom_call_target="tpu_custom_call" | custom-call | flops 754974720 | bytes 1179648 | tf_op jit(solution)/shard_map/pallas_call | solution.py:205
  30.5 3.8 %collective-permute-start.2 = (bf16[784,384]{1,0:T(8,128)(2,1)S(1)}, bf16[784,384]{1,0:T(8,128)(2,1)S(1)}, u32[]{:S(2)}, u32[]{:S(2)}) collective-permute-start(bf16[784,384]{1,0:T(8,128)(2,1)S(1)} %get-tuple-element.70), channel_id=1, source_target_pairs={{0,1},{1,0},{2,3},{3,2},{4,5},{5,4},{6,7},{7,6},{8,9},{9,8},{10,11... | collective-permute-start | bytes 1806344 | tf_op jit(solution)/shard_map/ppermute | solution.py:30
  34.2 1.6 %collective-permute-done.2 = bf16[784,384]{1,0:T(8,128)(2,1)S(1)} collective-permute-done((bf16[784,384]{1,0:T(8,128)(2,1)S(1)}, bf16[784,384]{1,0:T(8,128)(2,1)S(1)}, u32[]{:S(2)}, u32[]{:S(2)}) %collective-permute-start.2) | collective-permute-done | bytes 602144 | tf_op jit(solution)/shard_map/ppermute | solution.py:30
  36.1 0.9 pad_maximum_fusion
  37.0 3.5 %all-to-all-start = ((bf16[8,104,384]{2,1,0:T(8,128)(2,1)}), bf16[8,104,384]{2,1,0:T(8,128)(2,1)S(1)}, u32[]{:S(2)}, u32[]{:S(2)}) async-start(bf16[8,104,384]{2,1,0:T(8,128)(2,1)} %pad_maximum_fusion), calls=%async_computation | async-start | bytes 1277952 | tf_op jit(solution)/shard_map/all_to_all | solution.py:57
  40.8 1.8 %fusion.24 = f32[16,240,384]{2,1,0:T(8,128)S(1)} fusion(bf16[16,64,384]{2,1,0:T(8,128)(2,1)S(1)} %fusion, s32[64]{0:T(128)S(1)} %get-tuple-element.113, s32[64]{0:T(128)S(1)} %get-tuple-element.115, f32[16]{0:T(128)S(1)} %get-tuple-element.104, f32[16]{0:T(128)S(1)} %get-tuple-element.103, s32[240]{0:T(256)S(1)} %get-tuple-element.109, ...), kind=kOutput, calls=%fused_computation.70 | convolution fusion | flops 195133440 | bytes 6694432 | tf_op jit(solution)/shard_map/rmw,rmc->rwc/dot_general | solution.py:253
  43.4 8.2 %all-to-all-done = bf16[8,104,384]{2,1,0:T(8,128)(2,1)S(1)} async-done(((bf16[8,104,384]{2,1,0:T(8,128)(2,1)}), bf16[8,104,384]{2,1,0:T(8,128)(2,1)S(1)}, u32[]{:S(2)}, u32[]{:S(2)}) %all-to-all-start) | async-done | bytes 639008 | tf_op jit(solution)/shard_map/all_to_all | solution.py:57
  51.8 12.9 %all_to_all.25 = bf16[4,32,384]{2,1,0:T(8,128)(2,1)S(1)} all-to-all(bf16[4,32,384]{2,1,0:T(8,128)(2,1)S(1)} %pad_maximum_fusion.2), channel_id=1, replica_groups=mesh['x'=4,'z'=8,'yl'=2,'yh'=4,'core'=2] {'yh'}, dimensions={0} | all-to-all | bytes 196608 | tf_op jit(solution)/shard_map/all_to_all | solution.py:57
  65.4 3.4 %all-to-all-start.2 = ((bf16[8,32,384]{2,1,0:T(8,128)(2,1)}), bf16[8,32,384]{2,1,0:T(8,128)(2,1)S(1)}, u32[]{:S(2)}, u32[]{:S(2)}) async-start(bf16[8,32,384]{2,1,0:T(8,128)(2,1)} %broadcast_in_dim.71), calls=%async_computation.2 | async-start | bytes 393216 | tf_op jit(solution)/shard_map/all_to_all | solution.py:57
  68.8 6.0 %collective-permute-start.3 = (bf16[16,16,384]{2,1,0:T(8,128)(2,1)S(1)}, bf16[16,16,384]{2,1,0:T(8,128)(2,1)S(1)}, u32[]{:S(2)}, u32[]{:S(2)}) collective-permute-start(bf16[16,16,384]{2,1,0:T(8,128)(2,1)S(1)} %get-tuple-element.80), channel_id=1, source_target_pairs={{0,504},{8,0},{16,8},{24,16},{32,24},{40,32},{48,40},{56,48},{64,5... | collective-permute-start | bytes 589832 | tf_op jit(solution)/shard_map/ppermute | solution.py:26
  74.7 1.9 %collective-permute-start.4 = (bf16[16,16,384]{2,1,0:T(8,128)(2,1)S(1)}, bf16[16,16,384]{2,1,0:T(8,128)(2,1)S(1)}, u32[]{:S(2)}, u32[]{:S(2)}) collective-permute-start(bf16[16,16,384]{2,1,0:T(8,128)(2,1)S(1)} %get-tuple-element.81), channel_id=1, source_target_pairs={{0,8},{8,16},{16,24},{24,32},{32,40},{40,48},{48,56},{56,64},{64,7... | collective-permute-start | bytes 589832 | tf_op jit(solution)/shard_map/ppermute | solution.py:26
  78.0 3.3 %all-to-all-start.3 = ((bf16[4,24,384]{2,1,0:T(8,128)(2,1)}), bf16[4,24,384]{2,1,0:T(8,128)(2,1)S(1)}, u32[]{:S(2)}, u32[]{:S(2)}) async-start(bf16[4,24,384]{2,1,0:T(8,128)(2,1)} %broadcast_in_dim.72), calls=%async_computation.3 | async-start | bytes 147456 | tf_op jit(solution)/shard_map/all_to_all | solution.py:57
  82.5 3.1 %collective-permute-done.4 = bf16[16,16,384]{2,1,0:T(8,128)(2,1)S(1)} collective-permute-done((bf16[16,16,384]{2,1,0:T(8,128)(2,1)S(1)}, bf16[16,16,384]{2,1,0:T(8,128)(2,1)S(1)}, u32[]{:S(2)}, u32[]{:S(2)}) %collective-permute-start.4) | collective-permute-done | bytes 196640 | tf_op jit(solution)/shard_map/ppermute | solution.py:26
  85.6 2.9 %all-to-all-done.3 = bf16[4,24,384]{2,1,0:T(8,128)(2,1)S(1)} async-done(((bf16[4,24,384]{2,1,0:T(8,128)(2,1)}), bf16[4,24,384]{2,1,0:T(8,128)(2,1)S(1)}, u32[]{:S(2)}, u32[]{:S(2)}) %all-to-all-start.3) | async-done | bytes 73760 | tf_op jit(solution)/shard_map/all_to_all | solution.py:57
  88.5 10.5 %all_to_all.26 = bf16[8,96,384]{2,1,0:T(8,128)(2,1)S(1)} all-to-all(bf16[8,96,384]{2,1,0:T(8,128)(2,1)S(1)} %broadcast_in_dim.74), channel_id=1, replica_groups=mesh['x'=4,'z'=8,'yl'=2,'yh'=4,'core'=2] {'x','yl'}, dimensions={0} | all-to-all | bytes 1179648 | tf_op jit(solution)/shard_map/all_to_all | solution.py:57
  99.1 8.8 %collective-permute-start.5 = (bf16[768,384]{1,0:T(8,128)(2,1)S(1)}, bf16[768,384]{1,0:T(8,128)(2,1)S(1)}, u32[]{:S(2)}, u32[]{:S(2)}) collective-permute-start(bf16[768,384]{1,0:T(8,128)(2,1)S(1)} %bitcast.66), channel_id=1, source_target_pairs={{0,1},{1,0},{2,3},{3,2},{4,5},{5,4},{6,7},{7,6},{8,9},{9,8},{10,11... | collective-permute-start | bytes 1769480 | tf_op jit(solution)/shard_map/ppermute | solution.py:30
  108.0 0.7 fusion.19
  109.6 0.9 pad_maximum_fusion.1
  110.5 0.8 copy-done.3
  (62 shorter events, 8.0 us)
Async XLA Ops:
  0.6 19.2 %copy-start = (bf16[768,384]{1,0:T(8,128)(2,1)S(1)}, bf16[768,384]{1,0:T(8,128)(2,1)}, u32[]{:S(2)}) copy-start(bf16[768,384]{1,0:T(8,128)(2,1)} %param.23) | copy-start | bytes 1769476
  0.6 26.7 %copy-start.4 = (bf16[1,16,16,384]{3,2,1,0:T(8,128)(2,1)S(1)}, bf16[1,16,16,384]{3,2,1,0:T(8,128)(2,1)}, u32[]{:S(2)}) copy-start(bf16[1,16,16,384]{3,2,1,0:T(8,128)(2,1)} %param.16) | copy-start | bytes 589828
  0.7 20.6 %copy-start.6 = (s32[16]{0:T(128)S(1)}, s32[16]{0:T(128)}, u32[]{:S(2)}) copy-start(s32[16]{0:T(128)} %param.18) | copy-start | bytes 196
  0.7 21.2 %copy-start.5 = (f32[4,384]{1,0:T(4,128)S(1)}, f32[4,384]{1,0:T(4,128)}, u32[]{:S(2)}) copy-start(f32[4,384]{1,0:T(4,128)} %param.20) | copy-start | bytes 18436
  0.7 21.2 %collective-permute-start.1 = (bf16[16,16,384]{2,1,0:T(8,128)(2,1)}, bf16[16,16,384]{2,1,0:T(8,128)(2,1)S(1)}, u32[]{:S(2)}, u32[]{:S(2)}) collective-permute-start(bf16[16,16,384]{2,1,0:T(8,128)(2,1)} %bitcast.73), channel_id=1, source_target_pairs={{0,504},{8,0},{16,8},{24,16},{32,24},{40,32},{48,40},{56,48},{64,5... | collective-permute-start | bytes 589832 | tf_op jit(solution)/shard_map/ppermute | solution.py:26
  15.5 11.8 %collective-permute-start = (bf16[16,16,384]{2,1,0:T(8,128)(2,1)}, bf16[16,16,384]{2,1,0:T(8,128)(2,1)S(1)}, u32[]{:S(2)}, u32[]{:S(2)}) collective-permute-start(bf16[16,16,384]{2,1,0:T(8,128)(2,1)} %bitcast.74), channel_id=1, source_target_pairs={{0,8},{8,16},{16,24},{24,32},{32,40},{40,48},{48,56},{56,64},{64,7... | collective-permute-start | bytes 589832 | tf_op jit(solution)/shard_map/ppermute | solution.py:26
  21.1 6.2 %copy-start.1 = (bf16[1,16,16,384]{3,2,1,0:T(8,128)(2,1)S(1)}, bf16[1,16,16,384]{3,2,1,0:T(8,128)(2,1)}, u32[]{:S(2)}) copy-start(bf16[1,16,16,384]{3,2,1,0:T(8,128)(2,1)} %param.17) | copy-start | bytes 589828
  21.1 6.2 %copy-start.2 = (bf16[384,768]{1,0:T(8,128)(2,1)S(1)}, bf16[384,768]{1,0:T(8,128)(2,1)}, u32[]{:S(2)}) copy-start(bf16[384,768]{1,0:T(8,128)(2,1)} %win_hbm.1) | copy-start | bytes 1769476
  30.5 5.4 %collective-permute-start.2 = (bf16[784,384]{1,0:T(8,128)(2,1)S(1)}, bf16[784,384]{1,0:T(8,128)(2,1)S(1)}, u32[]{:S(2)}, u32[]{:S(2)}) collective-permute-start(bf16[784,384]{1,0:T(8,128)(2,1)S(1)} %get-tuple-element.70), channel_id=1, source_target_pairs={{0,1},{1,0},{2,3},{3,2},{4,5},{5,4},{6,7},{7,6},{8,9},{9,8},{10,11... | collective-permute-start | bytes 1806344 | tf_op jit(solution)/shard_map/ppermute | solution.py:30
  37.0 14.6 %all-to-all-start = ((bf16[8,104,384]{2,1,0:T(8,128)(2,1)}), bf16[8,104,384]{2,1,0:T(8,128)(2,1)S(1)}, u32[]{:S(2)}, u32[]{:S(2)}) async-start(bf16[8,104,384]{2,1,0:T(8,128)(2,1)} %pad_maximum_fusion), calls=%async_computation | async-start | bytes 1277952 | tf_op jit(solution)/shard_map/all_to_all | solution.py:57
  65.4 11.9 %all-to-all-start.2 = ((bf16[8,32,384]{2,1,0:T(8,128)(2,1)}), bf16[8,32,384]{2,1,0:T(8,128)(2,1)S(1)}, u32[]{:S(2)}, u32[]{:S(2)}) async-start(bf16[8,32,384]{2,1,0:T(8,128)(2,1)} %broadcast_in_dim.71), calls=%async_computation.2 | async-start | bytes 393216 | tf_op jit(solution)/shard_map/all_to_all | solution.py:57
  68.8 13.7 %collective-permute-start.3 = (bf16[16,16,384]{2,1,0:T(8,128)(2,1)S(1)}, bf16[16,16,384]{2,1,0:T(8,128)(2,1)S(1)}, u32[]{:S(2)}, u32[]{:S(2)}) collective-permute-start(bf16[16,16,384]{2,1,0:T(8,128)(2,1)S(1)} %get-tuple-element.80), channel_id=1, source_target_pairs={{0,504},{8,0},{16,8},{24,16},{32,24},{40,32},{48,40},{56,48},{64,5... | collective-permute-start | bytes 589832 | tf_op jit(solution)/shard_map/ppermute | solution.py:26
  74.7 10.8 %collective-permute-start.4 = (bf16[16,16,384]{2,1,0:T(8,128)(2,1)S(1)}, bf16[16,16,384]{2,1,0:T(8,128)(2,1)S(1)}, u32[]{:S(2)}, u32[]{:S(2)}) collective-permute-start(bf16[16,16,384]{2,1,0:T(8,128)(2,1)S(1)} %get-tuple-element.81), channel_id=1, source_target_pairs={{0,8},{8,16},{16,24},{24,32},{32,40},{40,48},{48,56},{56,64},{64,7... | collective-permute-start | bytes 589832 | tf_op jit(solution)/shard_map/ppermute | solution.py:26
  78.0 10.5 %all-to-all-start.3 = ((bf16[4,24,384]{2,1,0:T(8,128)(2,1)}), bf16[4,24,384]{2,1,0:T(8,128)(2,1)S(1)}, u32[]{:S(2)}, u32[]{:S(2)}) async-start(bf16[4,24,384]{2,1,0:T(8,128)(2,1)} %broadcast_in_dim.72), calls=%async_computation.3 | async-start | bytes 147456 | tf_op jit(solution)/shard_map/all_to_all | solution.py:57
  99.1 10.4 %collective-permute-start.5 = (bf16[768,384]{1,0:T(8,128)(2,1)S(1)}, bf16[768,384]{1,0:T(8,128)(2,1)S(1)}, u32[]{:S(2)}, u32[]{:S(2)}) collective-permute-start(bf16[768,384]{1,0:T(8,128)(2,1)S(1)} %bitcast.66), channel_id=1, source_target_pairs={{0,1},{1,0},{2,3},{3,2},{4,5},{5,4},{6,7},{7,6},{8,9},{9,8},{10,11... | collective-permute-start | bytes 1769480 | tf_op jit(solution)/shard_map/ppermute | solution.py:30
  110.5 0.8 copy-start.3
